TPU v7x, 32 devices: a whole 2x2x4 slice. The times are simulated.
32 devices in a mesh: group: 4 (over z), tp: 8 (over y, x, core).
Axes of the slice: x: 2, y: 2, z: 4, core: 2. Of those that a mesh axis runs over, the one named last changes fastest.
Arguments:
- tokens: bfloat16 [2048, 4096], P('group', 'tp'), may hold values from -6 to 6
- route_ids: int32 [2048, 2], P('group'), may hold values from 0 to 3, all different within a row; in each aligned block of 512 rows (0 to 511, 512 to 1023, ...) at most 320 rows name the same one
- route_weight: float32 [2048, 2], P('group'), may hold values from 0.25 to 4
- gate_weight: bfloat16 [4096, 6144], P(None, 'tp'), may hold values from -0.09375 to 0.09375
- up_weight: bfloat16 [4096, 6144], P(None, 'tp'), may hold values from -0.09375 to 0.09375
- down_weight: bfloat16 [6144, 4096], P('tp'), may hold values from -0.15625 to 0.15625
- gate_code: bfloat16 [4096, 6144], P('group', 'tp'), may hold values from -1 to 1
- up_code: bfloat16 [4096, 6144], P('group', 'tp'), may hold values from -1 to 1
- gate_scale: bfloat16 [32, 6144], P('group', 'tp'), may hold values from 0.0049743652 to 0.049804688
- up_scale: bfloat16 [32, 6144], P('group', 'tp'), may hold values from 0.0049743652 to 0.049804688
- down_code: bfloat16 [6144, 4096], P('tp', 'group'), may hold values from -1 to 1
- down_scale: bfloat16 [6144, 32], P('tp', 'group'), may hold values from 0.0079956055 to 0.079589844
Outputs:
- decoded: bfloat16 [2048, 4096], P('group', 'tp')
Inputs may be any that keep to these rules, and one draw needn't show every extreme that they name: `route_ids`: each token names 2 different experts; among the 512 tokens of one group no expert is named by more than 320 tokens.
All inputs are finite; a program needn't handle non-finite values.
Results may differ from a plain program's by a relative error of at most 0.007.
Values may be sent and summed in bfloat16 or wider, within the bound.
A program may use at most 128 MiB of HBM per device.

v0:
```python
import jax
import jax.numpy as jnp
from jax import lax
from jax.sharding import PartitionSpec as P

EXPERTS = 4


def refresh_rows(weight, code, scale):
    width = weight.shape[1]
    delta = (
        code.astype(jnp.float32).reshape(scale.shape[0], -1, width)
        * scale.astype(jnp.float32)[:, None, :]
    )
    return (weight.astype(jnp.float32) + delta.reshape(weight.shape)).astype(jnp.bfloat16)


def refresh_cols(weight, code, scale):
    height = weight.shape[0]
    delta = (
        code.astype(jnp.float32).reshape(height, scale.shape[1], -1)
        * scale.astype(jnp.float32)[:, :, None]
    )
    return (weight.astype(jnp.float32) + delta.reshape(weight.shape)).astype(jnp.bfloat16)


def slot_table(route_ids, combine, expert, capacity):
    token_count = route_ids.shape[0]
    named = route_ids == expert
    used = jnp.any(named, axis=1)
    weight_row = jnp.sum(jnp.where(named, combine, jnp.zeros_like(combine)), axis=1)
    place = jnp.cumsum(used.astype(jnp.int32)) - 1
    target = jnp.where(used, place, capacity)
    row_index = (
        jnp.zeros((capacity,), jnp.int32)
        .at[target]
        .set(jnp.arange(token_count, dtype=jnp.int32), mode="drop")
    )
    slot_weight = jnp.zeros((capacity,), jnp.float32).at[target].set(weight_row, mode="drop")
    return (row_index, slot_weight)


def body(
    tokens,
    route_ids,
    route_weight,
    gate_weight,
    up_weight,
    down_weight,
    gate_code,
    up_code,
    gate_scale,
    up_scale,
    down_code,
    down_scale,
):
    gate_full, up_full, gate_sfull, up_sfull = (
        lax.all_gather(gate_code, "group", axis=0, tiled=True),
        lax.all_gather(up_code, "group", axis=0, tiled=True),
        lax.all_gather(gate_scale, "group", axis=0, tiled=True),
        lax.all_gather(up_scale, "group", axis=0, tiled=True),
    )
    down_full, down_sfull = (
        lax.all_gather(down_code, "group", axis=1, tiled=True),
        lax.all_gather(down_scale, "group", axis=1, tiled=True),
    )
    gate_new = refresh_rows(gate_weight, gate_full, gate_sfull)
    up_new = refresh_rows(up_weight, up_full, up_sfull)
    down_new = refresh_cols(down_weight, down_full, down_sfull)
    features = lax.all_gather(tokens, "tp", axis=1, tiled=True)
    token_count = features.shape[0]
    capacity = token_count * route_ids.shape[1] * 5 // (EXPERTS * 4)
    share_count = lax.axis_size("tp") // EXPERTS
    combine = route_weight / jnp.sum(route_weight, axis=1, keepdims=True)
    expert = lax.axis_index("tp") // share_count
    row_index, slot_weight = slot_table(route_ids, combine, expert, capacity)
    picked = features[row_index]
    gate_value = jnp.dot(picked, gate_new, preferred_element_type=jnp.float32)
    up_value = jnp.dot(picked, up_new, preferred_element_type=jnp.float32)
    hidden = (jax.nn.silu(gate_value) * up_value).astype(jnp.bfloat16)
    term = jnp.dot(hidden, down_new, preferred_element_type=jnp.float32) * slot_weight[:, None]
    partial_value = jnp.zeros((token_count, features.shape[1]), jnp.float32).at[row_index].add(term)
    result = lax.psum_scatter(partial_value, "tp", scatter_dimension=1, tiled=True)
    return result.astype(jnp.bfloat16)


def solution(mesh):
    placed = (
        P("group", "tp"),
        P("group", None),
        P("group", None),
        P(None, "tp"),
        P(None, "tp"),
        P("tp", None),
        P("group", "tp"),
        P("group", "tp"),
        P("group", "tp"),
        P("group", "tp"),
        P("tp", "group"),
        P("tp", "group"),
    )
    return jax.shard_map(
        body, mesh=mesh, in_specs=placed, out_specs=P("group", "tp"), check_vma=False
    )
```

profile of v0, /device:TPU:0, one launch (start us, length us, event | category | flops | bytes accessed | tf_op | source)
XLA Modules:
  0.0 515.6 jit_solution(7690819886163229862)
XLA Ops:
  6.5 0.7 all-gather.5.cloned.1.call-update
  7.3 0.0 all-gather.7.cloned.1.call-start
  7.3 0.7 all-gather.7.cloned.1.call-update
  8.1 0.7 all-gather.9.cloned.1.call-update
  8.7 0.0 all-gather.11.cloned.1.call-start
  8.8 0.5 all-gather.11.cloned.1.call-update
  9.3 0.0 reduce-scatter.2.cloned.1.call-start
  9.4 0.7 fusion.26
  10.1 0.3 reduce-window.9
  10.4 0.1 slice.7
  10.5 0.7 reduce_sum.18
  11.2 0.1 slice_reduce_fusion
  11.3 0.7 fusion.20
  12.1 0.1 add_add_fusion
  12.2 2.4 scatter_custom_fusion.1
  14.6 2.4 scatter_custom_fusion
  17.0 15.0 %all_gather.23 = bf16[32,768]{1,0:T(8,128)(2,1)S(1)} all-gather(bf16[8,768]{1,0:T(8,128)(2,1)} %param.20), channel_id=1, replica_groups=mesh['group'=4,'tp'=8] {'group'}, dimensions={0}, use_global_device_ids=true | all-gather | bytes 61440 | tf_op jit(solution)/shard_map/all_gather | solution.py:60
  32.0 13.4 %all_gather.25 = bf16[32,768]{1,0:T(8,128)(2,1)S(1)} all-gather(bf16[8,768]{1,0:T(8,128)(2,1)} %param.21), channel_id=1, replica_groups=mesh['group'=4,'tp'=8] {'group'}, dimensions={0}, use_global_device_ids=true | all-gather | bytes 61440 | tf_op jit(solution)/shard_map/all_gather | solution.py:61
  45.4 13.5 %all_gather.27 = bf16[768,32]{0,1:T(8,128)(2,1)S(1)} all-gather(bf16[768,8]{0,1:T(8,128)(2,1)} %param.23), channel_id=1, replica_groups=mesh['group'=4,'tp'=8] {'group'}, dimensions={1}, use_global_device_ids=true | all-gather | bytes 61440 | tf_op jit(solution)/shard_map/all_gather | solution.py:65
  58.8 0.1 copy.14
  59.0 10.5 %gather_fusion = bf16[320,4096]{1,0:T(8,128)(2,1)S(1)} fusion(bf16[512,4096]{1,0:T(8,128)(2,1)} %all-gather.5.cloned.1.call-done, s32[1024]{0:T(1024)S(1)} %pad_clamp_fusion), kind=kCustom, calls=%fused_computation | custom fusion | bytes 5244160 | tf_op jit(solution)/shard_map/gather | solution.py:77
  69.6 96.8 %all-gather.7.cloned.1.call-done = bf16[4096,768]{1,0:T(8,128)(2,1)} async-done(((bf16[1024,768]{1,0:T(8,128)(2,1)}), bf16[4096,768]{1,0:T(8,128)(2,1)}) %all-gather.7.cloned.1.call-update) | async-done | bytes 6291472 | tf_op jit(solution)/shard_map/all_gather | solution.py:58
  166.4 9.3 %fusion.5 = bf16[4096,768]{1,0:T(8,128)(2,1)} fusion(bf16[4096,768]{1,0:T(8,128)(2,1)} %all-gather.7.cloned.1.call-done, bf16[4096,768]{1,0:T(8,128)(2,1)} %param.15, f32[32,768]{1,0:T(8,128)S(1)} %convert_element_type.53), kind=kLoop, calls=%fused_computation.12 | loop fusion | flops 15728640 | bytes 18972672 | tf_op jit(solution)/shard_map/convert_element_type | solution.py:15
  175.7 105.9 %all-gather.9.cloned.1.call-done = bf16[4096,768]{1,0:T(8,128)(2,1)} async-done(((bf16[1024,768]{1,0:T(8,128)(2,1)}), bf16[4096,768]{1,0:T(8,128)(2,1)}) %all-gather.9.cloned.1.call-update) | async-done | bytes 6291472 | tf_op jit(solution)/shard_map/all_gather | solution.py:59
  281.6 9.3 %fusion.3 = bf16[4096,768]{1,0:T(8,128)(2,1)} fusion(bf16[4096,768]{1,0:T(8,128)(2,1)} %all-gather.9.cloned.1.call-done, bf16[4096,768]{1,0:T(8,128)(2,1)} %param.16, f32[32,768]{1,0:T(8,128)S(1)} %convert_element_type.57), kind=kLoop, calls=%fused_computation.9 | loop fusion | flops 15728640 | bytes 18972672 | tf_op jit(solution)/shard_map/convert_element_type | solution.py:15
  290.8 6.5 %fusion.27 = f32[320,768]{1,0:T(8,128)} fusion(bf16[320,4096]{1,0:T(8,128)(2,1)S(1)} %gather_fusion, bf16[4096,768]{1,0:T(8,128)(2,1)} %fusion.5), kind=kOutput, calls=%fused_computation.41 | convolution fusion | flops 2013265920 | bytes 9895936 | tf_op jit(solution)/shard_map/dot_general | solution.py:78
  297.3 99.3 %all-gather.11.cloned.1.call-done = bf16[768,4096]{1,0:T(8,128)(2,1)} async-done(((bf16[768,1024]{1,0:T(8,128)(2,1)}), bf16[768,4096]{1,0:T(8,128)(2,1)}) %all-gather.11.cloned.1.call-update) | async-done | bytes 6291472 | tf_op jit(solution)/shard_map/all_gather | solution.py:64
  396.6 7.2 %mul.56 = f32[768,32,128]{2,1,0:T(8,128)} broadcast(f32[768,32]{1,0:T(8,128)S(1)} %copy.14), dimensions={0,1} | broadcast | bytes 12681216 | tf_op jit(solution)/shard_map/mul | solution.py:21
  403.8 20.4 %fusion.8 = f32[320,4096]{1,0:T(8,128)} fusion(f32[96,8,32,128]{3,2,1,0:T(8,128)} %bitcast.32, bf16[768,4096]{1,0:T(8,128)(2,1)} %all-gather.11.cloned.1.call-done, bf16[768,4096]{1,0:T(8,128)(2,1)} %param.17, f32[320]{0:T(512)S(1)} %scatter_custom_fusion.1, bf16[320,4096]{1,0:T(8,128)(2,1)S(1)} %gather_fusion, bf16[4096,768]{1,0:T(8,128)(2,1)} %fusion.3, ...), kind=kOutput, calls=%fused_computation.14 | convolution fusion | flops 4045045760 | bytes 40305920 | tf_op jit(solution)/shard_map/dot_general | solution.py:81
  424.2 13.1 %scatter_custom_fusion.2 = f32[512,4096]{1,0:T(8,128)} fusion(s32[320]{0:T(512)S(1)} %compare_select_fusion.1, f32[320,4096]{1,0:T(8,128)} %fusion.8, f32[]{:T(128)} %constant.13.clone.1), kind=kCustom, calls=%fused_computation.15 | custom fusion | flops 1310720 | bytes 8389120 | tf_op jit(solution)/shard_map/scatter-add | solution.py:82
  437.3 69.6 %reduce-scatter.2.cloned.1.call-done = f32[512,512]{1,0:T(8,128)} async-done(((f32[512,4096]{1,0:T(8,128)}), f32[512,512]{1,0:T(8,128)}) %reduce-scatter.2.cloned.1.call-update) | async-done | bytes 1048592 | tf_op jit(solution)/shard_map/reduce_scatter | solution.py:83
  507.0 2.1 convert_element_type.64
  (12 shorter events, 0.2 us)
Async XLA Ops:
  6.5 52.5 %all-gather.5.cloned.1.call-start = ((), (), s32[]{:S(2)}) async-start(), calls=%async_computation.1 | async-start | bytes 4718592 | tf_op jit(solution)/shard_map/all_gather | solution.py:70
  7.3 159.1 %all-gather.7.cloned.1.call-start = ((), (), s32[]{:S(2)}) async-start(), calls=%async_computation.2 | async-start | bytes 7864320 | tf_op jit(solution)/shard_map/all_gather | solution.py:58
  8.0 273.5 %all-gather.9.cloned.1.call-start = ((), (), s32[]{:S(2)}) async-start(), calls=%async_computation.3 | async-start | bytes 7864320 | tf_op jit(solution)/shard_map/all_gather | solution.py:59
  8.7 387.9 %all-gather.11.cloned.1.call-start = ((), (), s32[]{:S(2)}) async-start(), calls=%async_computation.4 | async-start | bytes 7864320 | tf_op jit(solution)/shard_map/all_gather | solution.py:64
  9.3 497.6 %reduce-scatter.2.cloned.1.call-start = ((), (), s32[]{:S(2)}) async-start(), calls=%async_computation.5 | async-start | bytes 9437184 | tf_op jit(solution)/shard_map/reduce_scatter | solution.py:83
Sparse Core Ops, SparseCore 0:
  9.2 40.1 all-gather.4
  51.0 115.3 all-gather.6
  167.9 113.5 all-gather.8
  283.0 113.5 all-gather.10
  437.5 69.4 reduce-scatter.1
where the time goes:
time: 516 us
  waiting for transfers between devices  374 us (72%)
  blocking collectives  41.8 us (8%)
  other arithmetic  36.4 us (7%)
  matrix products  26.9 us (5%)
  local copies, waits for them, and re-layouts  23 us (4%)
  between operations  13.2 us (3%)
    all_gather x1, waiting for transfers between devices, body(): lax.all_gather(up_code, 'group', axis=0, tiled=True)  106 us
    all_gather x1, waiting for transfers between devices, body(): lax.all_gather(down_code, 'group', axis=1, tiled=True)  99.3 us
    all_gather x1, waiting for transfers between devices, body(): lax.all_gather(gate_code, 'group', axis=0, tiled=True)  96.8 us
    reduce_scatter x1, waiting for transfers between devices, body(): lax.psum_scatter(partial_value, 'tp', scatter_dimension=1, tiled=True)  69.6 us
    dot_general x1, matrix products, body(): jnp.dot(hidden, down_new, preferred_element_type=jnp.float32)  20.4 us
    convert_element_type x2, other arithmetic, refresh_rows(): (weight.astype(jnp.float32) + delta.reshape(weight.shape)).astype(jnp.bfl...  18.6 us
    all_gather x1, blocking collectives, body(): lax.all_gather(gate_scale, 'group', axis=0, tiled=True)  15 us
    all_gather x1, blocking collectives, body(): lax.all_gather(down_scale, 'group', axis=1, tiled=True)  13.5 us
  transfers between devices with their start and end apart: 5, of which 4 were waited for; matrix products, arithmetic and copies ran while one was open for 8% of the time, Pallas kernels for 0%

commit v1 on v0

v1 whole, which is shorter than its diff:
```python
import jax
import jax.numpy as jnp
from jax import lax
from jax.sharding import PartitionSpec as P

EXPERTS = 4


def refresh_rows(weight, code, scale):
    width = weight.shape[1]
    delta = (
        code.astype(jnp.float32).reshape(scale.shape[0], -1, width)
        * scale.astype(jnp.float32)[:, None, :]
    )
    return (weight.astype(jnp.float32) + delta.reshape(weight.shape)).astype(jnp.bfloat16)


def refresh_cols(weight, code, scale):
    height = weight.shape[0]
    delta = (
        code.astype(jnp.float32).reshape(height, scale.shape[1], -1)
        * scale.astype(jnp.float32)[:, :, None]
    )
    return (weight.astype(jnp.float32) + delta.reshape(weight.shape)).astype(jnp.bfloat16)


def body(
    tokens,
    route_ids,
    route_weight,
    gate_weight,
    up_weight,
    down_weight,
    gate_code,
    up_code,
    gate_scale,
    up_scale,
    down_code,
    down_scale,
):
    groups, share = lax.axis_size("group"), lax.axis_size("tp")
    group = lax.axis_index("group")
    rows, part = tokens.shape
    width = part * share
    depth = width // groups
    columns = down_code.shape[1]
    capacity = rows * route_ids.shape[1] * 5 // (EXPERTS * 4)
    expert = lax.axis_index("tp") // (share // EXPERTS)

    mine = lax.all_to_all(tokens, "tp", split_axis=0, concat_axis=1, tiled=True)
    mine = mine.reshape(rows // share, groups, depth).transpose(1, 0, 2)
    mine = lax.all_to_all(mine, "group", split_axis=0, concat_axis=0, tiled=True)
    every = lax.all_gather(mine, "tp", axis=1, tiled=True)

    combine = route_weight / jnp.sum(route_weight, axis=1, keepdims=True)
    named = route_ids == expert
    weight_row = jnp.sum(jnp.where(named, combine, jnp.zeros_like(combine)), axis=1)
    used = jnp.any(named, axis=1)
    place = jnp.cumsum(used.astype(jnp.int32)) - 1
    target = jnp.where(used, place, capacity)
    both = jnp.stack([target.astype(jnp.float32), weight_row], axis=0)
    both = lax.all_gather(both, "group", axis=0, tiled=False)
    target_all = both[:, 0].astype(jnp.int32)
    pick = target_all[:, None, :] == lax.broadcasted_iota(jnp.int32, (groups, capacity, rows), 1)
    slot_weight = jnp.sum(jnp.where(pick, both[:, 1][:, None, :], 0.0), axis=2)
    pick = pick.astype(jnp.bfloat16)

    picked = jnp.einsum("gsn,gnk->gsk", pick, every)
    picked = picked.reshape(groups * capacity, depth)

    gate_new = refresh_rows(
        lax.dynamic_slice_in_dim(gate_weight, group * depth, depth, 0), gate_code, gate_scale
    )
    up_new = refresh_rows(
        lax.dynamic_slice_in_dim(up_weight, group * depth, depth, 0), up_code, up_scale
    )
    down_new = refresh_cols(
        lax.dynamic_slice_in_dim(down_weight, group * columns, columns, 1), down_code, down_scale
    )
    both_new = jnp.concatenate([gate_new, up_new], axis=1)
    value = jnp.dot(picked, both_new, preferred_element_type=jnp.float32).astype(jnp.bfloat16)
    value = value.reshape(groups, capacity, -1)
    value = lax.all_to_all(value, "group", split_axis=0, concat_axis=0, tiled=True)
    value = jnp.sum(value.astype(jnp.float32), axis=0)
    half = value.shape[1] // 2
    hidden = (jax.nn.silu(value[:, :half]) * value[:, half:]).astype(jnp.bfloat16)

    hidden_all = lax.all_gather(hidden, "group", axis=0, tiled=True)
    term = jnp.dot(hidden_all, down_new, preferred_element_type=jnp.float32)
    term = (term.reshape(groups, capacity, columns) * slot_weight[:, :, None]).astype(jnp.bfloat16)
    spread = jnp.einsum("gsn,gsk->gnk", pick, term)
    spread = spread.reshape(groups, share, rows // share, columns).transpose(1, 0, 2, 3)
    total = lax.psum_scatter(spread, "tp", scatter_dimension=0, tiled=True)[0]
    total = lax.all_to_all(total, "group", split_axis=0, concat_axis=0, tiled=True)
    total = total.transpose(1, 0, 2).reshape(rows // share, width)
    return lax.all_to_all(total, "tp", split_axis=1, concat_axis=0, tiled=True).astype(jnp.bfloat16)


def solution(mesh):
    placed = (
        P("group", "tp"),
        P("group", None),
        P("group", None),
        P(None, "tp"),
        P(None, "tp"),
        P("tp", None),
        P("group", "tp"),
        P("group", "tp"),
        P("group", "tp"),
        P("group", "tp"),
        P("tp", "group"),
        P("tp", "group"),
    )
    return jax.shard_map(
        body, mesh=mesh, in_specs=placed, out_specs=P("group", "tp"), check_vma=False
    )
```

time: 516 us -> 321 us (0.62)
  waiting for transfers between devices: 374 us -> 108 us
  blocking collectives: 41.8 us -> 171 us
  other arithmetic: 36.4 us -> 7.11 us
  local copies, waits for them, and re-layouts: 23 us -> 6.53 us
  matrix products: 26.9 us -> 14.7 us
    all_gather x4 -> x2, waiting for transfers between devices: 302 us -> 57.4 us  [the longest x1 41.1 us: body(): hidden_all = lax.all_gather(hidden, 'group', axis=0, tiled=True)]
    all_to_all x0 -> x5, blocking collectives: none -> 157 us  [the longest x1 92.4 us: body(): lax.all_to_all(value, 'group', split_axis=0, concat_axis=0, tiled=True)]
    all_gather x3 -> x1, blocking collectives: 41.8 us -> 13.1 us  [body(): both = lax.all_gather(both, 'group', axis=0, tiled=False)]
    reduce_scatter x1, waiting for transfers between devices: 69.6 us -> 50.3 us  [body(): total = lax.psum_scatter(spread, 'tp', scatter_dimension=0, tiled=True)[0]]
    convert_element_type x2 -> x1, other arithmetic: 18.6 us -> 4.53 us  [refresh_rows(): (weight.astype(jnp.float32) + delta.reshape(weight.shape)).astype(jnp.bfl...]
    scatter-add x1 -> x0, other arithmetic: 13.1 us -> none  [body(): jnp.zeros((token_count, features.shape[1]), jnp.float32).at[row_index]]
    dot_general x2 -> x4, matrix products: 26.9 us -> 14.7 us  [the longest x1 4.66 us: body(): jnp.dot(picked, both_new, preferred_element_type=jnp.float32)]
    gather x1 -> x0, local copies, waits for them, and re-layouts: 10.5 us -> none  [body(): picked = features[row_index]]
  transfers between devices with their start and end apart: 5 -> 3, of which waited for: 4 -> 3; matrix products, arithmetic and copies ran while one was open for 8% -> 2% of each run, Pallas kernels for 0% -> 0%
where the time goes in v1:
time: 321 us; the launch traced here: 320 us
  blocking collectives  171 us (53%)
  waiting for transfers between devices  108 us (34%)
  matrix products  14.7 us (5%)
  between operations  13.3 us (4%)
  other arithmetic  7.11 us (2%)
  local copies, waits for them, and re-layouts  6.53 us (2%)
    all_to_all x1, blocking collectives, body(): lax.all_to_all(value, 'group', split_axis=0, concat_axis=0, tiled=True)  92.4 us
    reduce_scatter x1, waiting for transfers between devices, body(): total = lax.psum_scatter(spread, 'tp', scatter_dimension=0, tiled=True)[0]  50.3 us
    all_gather x1, waiting for transfers between devices, body(): hidden_all = lax.all_gather(hidden, 'group', axis=0, tiled=True)  41.1 us
    all_to_all x1, blocking collectives, body(): lax.all_to_all(total, 'group', split_axis=0, concat_axis=0, tiled=True)  19.1 us
    all_to_all x1, blocking collectives, body(): lax.all_to_all(mine, 'group', split_axis=0, concat_axis=0, tiled=True)  18.6 us
    all_gather x1, waiting for transfers between devices, body(): every = lax.all_gather(mine, 'tp', axis=1, tiled=True)  16.3 us
    all_to_all x1, blocking collectives, body(): mine = lax.all_to_all(tokens, 'tp', split_axis=0, concat_axis=1, tiled=True)  15.1 us
    all_gather x1, blocking collectives, body(): both = lax.all_gather(both, 'group', axis=0, tiled=False)  13.1 us
  transfers between devices with their start and end apart: 3, of which 3 were waited for; matrix products, arithmetic and copies ran while one was open for 2% of the time, Pallas kernels for 0%

profile of v1, /device:TPU:0, one launch (start us, length us, event | category | flops | bytes accessed | tf_op | source)
XLA Modules:
  0.0 320.3 jit_solution(13925218058692638813)
XLA Ops:
  6.6 15.1 %all_to_all.50 = bf16[8,64,512]{2,1,0:T(8,128)(2,1)S(1)} all-to-all(bf16[8,64,512]{2,1,0:T(8,128)(2,1)} %bitcast.61), channel_id=1, replica_groups=mesh['group'=4,'tp'=8] {'tp'}, dimensions={0} | all-to-all | bytes 1048576 | tf_op jit(solution)/shard_map/all_to_all | solution.py:50
  21.6 0.3 copy.23
  21.9 0.3 reshape.86
  22.3 0.2 copy.39
  22.4 18.6 %all_to_all.51 = bf16[4,64,1024]{2,1,0:T(8,128)(2,1)} all-to-all(bf16[4,64,1024]{2,1,0:T(8,128)(2,1)S(1)} %bitcast.57), channel_id=1, replica_groups=mesh['group'=4,'tp'=8] {'group'}, dimensions={0} | all-to-all | bytes 1048576 | tf_op jit(solution)/shard_map/all_to_all | solution.py:52
  41.2 0.3 reduce-window.9
  41.5 0.1 slice.19
  41.6 0.1 slice_reduce_fusion
  41.9 13.1 %all-gather.1 = f32[4,2,512]{2,1,0:T(2,128)S(1)} all-gather(f32[1,2,512]{2,1,0:T(2,128)S(1)} %maximum_bitcast_fusion), channel_id=2, replica_groups=mesh['group'=4,'tp'=8] {'group'}, dimensions={0}, use_global_device_ids=true | all-gather | bytes 20480 | tf_op jit(solution)/shard_map/all_gather | solution.py:62
  55.1 4.5 %fusion.6 = (bf16[1024,768]{1,0:T(8,128)(2,1)S(1)}, bf16[1024,768]{1,0:T(8,128)(2,1)}) fusion(bf16[1024,768]{1,0:T(8,128)(2,1)S(1)} %copy-done, f32[8,768]{1,0:T(8,128)S(1)} %convert_element_type.80, bf16[4096,768]{1,0:T(8,128)(2,1)} %param.16, s32[]{:T(128)S(6)} %select_n.32, f32[8,768]{1,0:T(8,128)S(1)} %convert_element_type.76, ...), kind=kLoop, calls=%fused_computation.12 | loop fusion | flops 7864320 | bytes 9486340 | tf_op jit(solution)/shard_map/convert_element_type | solution.py:15
  59.6 16.3 %all-gather.5.cloned.1.call-done = bf16[4,512,1024]{2,1,0:T(8,128)(2,1)} async-done(((bf16[4,64,1024]{2,1,0:T(8,128)(2,1)}), bf16[4,512,1024]{2,1,0:T(8,128)(2,1)}) %all-gather.5.cloned.1.call-update) | async-done | bytes 4194320 | tf_op jit(solution)/shard_map/all_gather | solution.py:53
  75.9 3.8 %fusion.11 = bf16[4,320,1024]{2,1,0:T(8,128)(2,1)S(1)} fusion(bf16[4,512,1024]{2,1,0:T(8,128)(2,1)} %all-gather.5.cloned.1.call-done, s32[4,512]{1,0:T(4,128)S(1)} %bitcast.63), kind=kOutput, calls=%fused_computation.20 | convolution fusion | flops 1342832640 | bytes 6823936 | tf_op jit(solution)/shard_map/gsn,gnk->gsk/dot_general | solution.py:68
  79.8 4.7 %convolution_convert_fusion = bf16[1280,1536]{1,0:T(8,128)(2,1)S(1)} fusion(bf16[1280,1024]{1,0:T(8,128)(2,1)S(1)} %bitcast.69, bf16[1024,768]{1,0:T(8,128)(2,1)S(1)} %get-tuple-element.7, bf16[1024,768]{1,0:T(8,128)(2,1)S(1)} %copy-done.1), kind=kOutput, calls=%fused_computation.1 | convolution fusion | flops 4034789376 | bytes 9699328 | tf_op jit(solution)/shard_map/dot_general | solution.py:81
  84.5 92.4 %all_to_all.52 = bf16[4,320,1536]{2,1,0:T(8,128)(2,1)S(1)} all-to-all(bf16[4,320,1536]{2,1,0:T(8,128)(2,1)S(1)} %bitcast.55), channel_id=1, replica_groups=mesh['group'=4,'tp'=8] {'group'}, dimensions={0} | all-to-all | bytes 7864320 | tf_op jit(solution)/shard_map/all_to_all | solution.py:83
  176.8 0.6 convert_reduce_fusion
  177.4 1.1 fusion.17
  178.5 0.2 reduce-scatter.2.cloned.1.call-start
  178.8 0.1 copy.25
  178.9 0.4 select_reduce_fusion
  179.3 41.1 %all-gather.7.cloned.1.call-done = bf16[1280,768]{1,0:T(8,128)(2,1)} async-done(((bf16[320,768]{1,0:T(8,128)(2,1)}), bf16[1280,768]{1,0:T(8,128)(2,1)}) %all-gather.7.cloned.1.call-update) | async-done | bytes 1966096 | tf_op jit(solution)/shard_map/all_gather | solution.py:88
  220.4 0.9 mul.62
  221.3 0.7 copy-done.7
  221.9 3.7 %fusion.12 = f32[1280,1024]{1,0:T(8,128)S(1)} fusion(bf16[1280,768]{1,0:T(8,128)(2,1)S(1)} %copy-done.7, f32[96,8,8,128]{3,2,1,0:T(8,128)S(1)} %bitcast.56, bf16[768,1024]{1,0:T(8,128)(2,1)S(1)} %copy-done.8, bf16[768,4096]{1,0:T(8,128)(2,1)} %param.17, s32[]{:T(128)S(6)} %select_n.32), kind=kOutput, calls=%fused_computation.21 | convolution fusion | flops 2017198080 | bytes 13500420 | tf_op jit(solution)/shard_map/dot_general | solution.py:89
  225.7 2.5 fusion.9
  228.2 2.4 copy.38
  230.6 50.3 %reduce-scatter.2.cloned.1.call-done = bf16[1,4,64,1024]{3,2,1,0:T(8,128)(2,1)} async-done(((bf16[8,4,64,1024]{3,2,1,0:T(8,128)(2,1)}), bf16[1,4,64,1024]{3,2,1,0:T(8,128)(2,1)}) %reduce-scatter.2.cloned.1.call-update) | async-done | bytes 524304 | tf_op jit(solution)/shard_map/reduce_scatter | solution.py:93
  280.9 19.1 %all_to_all.53 = bf16[4,64,1024]{2,1,0:T(8,128)(2,1)S(1)} all-to-all(bf16[4,64,1024]{2,1,0:T(8,128)(2,1)} %bitcast.62), channel_id=1, replica_groups=mesh['group'=4,'tp'=8] {'group'}, dimensions={0} | all-to-all | bytes 1048576 | tf_op jit(solution)/shard_map/all_to_all | solution.py:94
  300.0 0.4 copy.27
  300.4 0.1 all_to_all.41
  300.5 0.2 copy.28
  300.7 12.3 %all_to_all.54 = bf16[64,8,512]{2,0,1:T(8,128)(2,1)S(1)} all-to-all(bf16[64,8,512]{2,0,1:T(8,128)(2,1)S(1)} %copy.28), channel_id=1, replica_groups=mesh['group'=4,'tp'=8] {'tp'}, dimensions={1} | all-to-all | bytes 1048576 | tf_op jit(solution)/shard_map/all_to_all | solution.py:96
  312.9 0.8 copy.43
  (35 shorter events, 0.4 us)
Async XLA Ops:
  6.5 34.6 %copy-start.2 = (s32[512,2]{0,1:T(2,128)S(1)}, s32[512,2]{0,1:T(2,128)}, u32[]{:S(2)}) copy-start(s32[512,2]{0,1:T(2,128)} %param.13) | copy-start | bytes 12292
  6.5 35.1 %copy-start.3 = (f32[512,2]{0,1:T(2,128)S(1)}, f32[512,2]{0,1:T(2,128)}, u32[]{:S(2)}) copy-start(f32[512,2]{0,1:T(2,128)} %param.14) | copy-start | bytes 12292
  6.5 48.5 %copy-start.5 = (bf16[8,768]{1,0:T(8,128)(2,1)S(1)}, bf16[8,768]{1,0:T(8,128)(2,1)}, u32[]{:S(2)}) copy-start(bf16[8,768]{1,0:T(8,128)(2,1)} %param.20) | copy-start | bytes 36868
  6.5 48.5 %copy-start.6 = (bf16[8,768]{1,0:T(8,128)(2,1)S(1)}, bf16[8,768]{1,0:T(8,128)(2,1)}, u32[]{:S(2)}) copy-start(bf16[8,768]{1,0:T(8,128)(2,1)} %param.21) | copy-start | bytes 36868
  6.5 48.5 %copy-start = (bf16[1024,768]{1,0:T(8,128)(2,1)S(1)}, bf16[1024,768]{1,0:T(8,128)(2,1)}, u32[]{:S(2)}) copy-start(bf16[1024,768]{1,0:T(8,128)(2,1)} %param.19) | copy-start | bytes 4718596
  6.5 69.4 %all-gather.5.cloned.1.call-start = ((), (), s32[]{:S(2)}) async-start(), calls=%async_computation.6 | async-start | bytes 4718592 | tf_op jit(solution)/shard_map/all_gather | solution.py:53
  41.1 179.3 %all-gather.7.cloned.1.call-start = ((), (), s32[]{:S(2)}) async-start(), calls=%async_computation.7 | async-start | bytes 2457600 | tf_op jit(solution)/shard_map/all_gather | solution.py:88
  75.9 3.8 %copy-start.1 = (bf16[1024,768]{1,0:T(8,128)(2,1)S(1)}, bf16[1024,768]{1,0:T(8,128)(2,1)}, u32[]{:S(2)}) copy-start(bf16[1024,768]{1,0:T(8,128)(2,1)} %get-tuple-element.8) | copy-start | bytes 4718596
  176.8 2.0 copy-start.4
  177.4 43.8 %copy-start.8 = (bf16[768,1024]{1,0:T(8,128)(2,1)S(1)}, bf16[768,1024]{1,0:T(8,128)(2,1)}, u32[]{:S(2)}) copy-start(bf16[768,1024]{1,0:T(8,128)(2,1)} %param.22) | copy-start | bytes 4718596
  178.5 102.3 %reduce-scatter.2.cloned.1.call-start = ((), (), s32[]{:S(2)}) async-start(), calls=%async_computation.8 | async-start | bytes 4718592 | tf_op jit(solution)/shard_map/reduce_scatter | solution.py:93
  220.4 1.5 copy-start.7
Sparse Core Ops, SparseCore 0:
  41.2 34.6 all-gather.4
  178.7 41.6 all-gather.6
  230.7 50.1 reduce-scatter.1

commit v2 on v1

--- a/solution.py
+++ b/solution.py
@@ -1,9 +1,190 @@
+import functools
+
 import jax
 import jax.numpy as jnp
 from jax import lax
+from jax.experimental import pallas as pl
+from jax.experimental.pallas import tpu as pltpu
 from jax.sharding import PartitionSpec as P
 
 EXPERTS = 4
+CHUNK = 64
+
+
+def expert_kernel(
+    groups,
+    chunk,
+    x_ref,
+    w_ref,
+    down_ref,
+    weight_ref,
+    term_ref,
+    out_up,
+    out_low,
+    in_up,
+    in_low,
+    hidden,
+    sem,
+):
+    me = lax.axis_index("group")
+    last = groups - 1
+    half = x_ref.shape[0] // 2
+    count = half // chunk
+    width = w_ref.shape[1] // 2
+
+    barrier = pltpu.get_barrier_semaphore()
+
+    @pl.when(me > 0)
+    def _():
+        pl.semaphore_signal(
+            barrier, inc=1, device_id={"group": me - 1}, device_id_type=pl.DeviceIdType.MESH
+        )
+
+    @pl.when(me < last)
+    def _():
+        pl.semaphore_signal(
+            barrier, inc=1, device_id={"group": me + 1}, device_id_type=pl.DeviceIdType.MESH
+        )
+
+    @pl.when((me > 0) & (me < last))
+    def _():
+        pl.semaphore_wait(barrier, 2)
+
+    @pl.when((me == 0) | (me == last))
+    def _():
+        pl.semaphore_wait(barrier, 1)
+
+    def piece(k, start):
+        return pl.ds(pl.multiple_of(start + k * chunk, chunk), chunk)
+
+    def move(k, source, target, number, where):
+        return pltpu.make_async_remote_copy(
+            src_ref=source,
+            dst_ref=target,
+            send_sem=sem.at[number, k],
+            recv_sem=sem.at[number + 1, k],
+            device_id={"group": where},
+            device_id_type=pl.DeviceIdType.MESH,
+        )
+
+    def sum_move(k, upward):
+        if upward:
+            return move(k, out_up.at[piece(k, 0)], in_up.at[piece(k, 0)], 0, lax.rem(me + 1, groups))
+        return move(k, out_low.at[piece(k, 0)], in_low.at[piece(k, 0)], 2, lax.rem(me + last, groups))
+
+    def hidden_move(k, upward):
+        if upward:
+            return move(k, hidden.at[piece(k, half)], hidden.at[piece(k, half)], 4, lax.rem(me + last, groups))
+        return move(k, hidden.at[piece(k, 0)], hidden.at[piece(k, 0)], 6, lax.rem(me + 1, groups))
+
+    def finish(k, start):
+        rows = piece(k, start)
+        term = jnp.dot(hidden[rows, :], down_ref[...], preferred_element_type=jnp.float32)
+        term_ref[rows, :] = (term * weight_ref[rows, :]).astype(jnp.bfloat16)
+
+    def add(k, upward):
+        start = half if upward else 0
+        first, final = (0, last) if upward else (last, 0)
+        inside, outside = (in_up, out_up) if upward else (in_low, out_low)
+        here = piece(k, 0)
+        own = jnp.dot(x_ref[piece(k, start), :], w_ref[...], preferred_element_type=jnp.float32)
+
+        @pl.when(me == first)
+        def _():
+            outside[here, :] = own.astype(jnp.bfloat16)
+
+        @pl.when(me != first)
+        def _():
+            sum_move(k, upward).wait_recv()
+
+            @pl.when(me != final)
+            def _():
+                outside[here, :] = (own + inside[here, :].astype(jnp.float32)).astype(jnp.bfloat16)
+
+            @pl.when(me == final)
+            def _():
+                value = own + inside[here, :].astype(jnp.float32)
+                gate, up = value[:, :width], value[:, width:]
+                hidden[piece(k, start), :] = (gate / (1.0 + jnp.exp(-gate)) * up).astype(
+                    jnp.bfloat16
+                )
+
+        @pl.when(me != final)
+        def _():
+            sum_move(k, upward).start()
+
+        @pl.when(me == final)
+        def _():
+            hidden_move(k, upward).start()
+            finish(k, start)
+
+    def take(k, upward):
+        final, end = (last, 0) if upward else (0, last)
+        hidden_move(k, upward).wait_recv()
+
+        @pl.when(me != end)
+        def _():
+            hidden_move(k, upward).start()
+
+        finish(k, half if upward else 0)
+
+    def step(t, _):
+        for upward in (True, False):
+            place = me if upward else last - me
+            k = t - place
+
+            @pl.when((k >= 0) & (k < count))
+            def _():
+                add(k, upward)
+
+        for upward in (True, False):
+            place = me if upward else last - me
+            j = t - (2 * last - place)
+
+            @pl.when((j >= 0) & (j < count) & (place != last))
+            def _():
+                take(j, upward)
+
+        return 0
+
+    lax.fori_loop(0, count + 2 * last, step, 0)
+
+    def settle(k, _):
+        for upward in (True, False):
+            final, end = (last, 0) if upward else (0, last)
+
+            @pl.when(me != final)
+            def _():
+                sum_move(k, upward).wait_send()
+
+            @pl.when(me != end)
+            def _():
+                hidden_move(k, upward).wait_send()
+
+        return 0
+
+    lax.fori_loop(0, count, settle, 0)
+
+
+def expert_terms(groups, picked, both_new, down_new, slot_weight):
+    rows, columns = picked.shape[0], down_new.shape[1]
+    half, width = rows // 2, down_new.shape[0]
+    chunk = CHUNK
+    vmem = pl.BlockSpec(memory_space=pltpu.VMEM)
+    return pl.pallas_call(
+        functools.partial(expert_kernel, groups, chunk),
+        out_shape=jax.ShapeDtypeStruct((rows, columns), jnp.bfloat16),
+        in_specs=[vmem] * 4,
+        out_specs=vmem,
+        scratch_shapes=[
+            *[pltpu.VMEM((half, 2 * width), jnp.bfloat16)] * 4,
+            pltpu.VMEM((rows, width), jnp.bfloat16),
+            pltpu.SemaphoreType.DMA((8, half // chunk)),
+        ],
+        compiler_params=pltpu.CompilerParams(
+            collective_id=0, has_side_effects=True, vmem_limit_bytes=48 * 1024 * 1024
+        ),
+    )(picked, both_new, down_new, slot_weight)
 
 
 def refresh_rows(weight, code, scale):
@@ -78,16 +259,8 @@
         lax.dynamic_slice_in_dim(down_weight, group * columns, columns, 1), down_code, down_scale
     )
     both_new = jnp.concatenate([gate_new, up_new], axis=1)
-    value = jnp.dot(picked, both_new, preferred_element_type=jnp.float32).astype(jnp.bfloat16)
-    value = value.reshape(groups, capacity, -1)
-    value = lax.all_to_all(value, "group", split_axis=0, concat_axis=0, tiled=True)
-    value = jnp.sum(value.astype(jnp.float32), axis=0)
-    half = value.shape[1] // 2
-    hidden = (jax.nn.silu(value[:, :half]) * value[:, half:]).astype(jnp.bfloat16)
-
-    hidden_all = lax.all_gather(hidden, "group", axis=0, tiled=True)
-    term = jnp.dot(hidden_all, down_new, preferred_element_type=jnp.float32)
-    term = (term.reshape(groups, capacity, columns) * slot_weight[:, :, None]).astype(jnp.bfloat16)
+    term = expert_terms(groups, picked, both_new, down_new, slot_weight.reshape(-1, 1))
+    term = term.reshape(groups, capacity, columns)
     spread = jnp.einsum("gsn,gsk->gnk", pick, term)
     spread = spread.reshape(groups, share, rows // share, columns).transpose(1, 0, 2, 3)
     total = lax.psum_scatter(spread, "tp", scatter_dimension=0, tiled=True)[0]

time: 321 us -> 270 us (0.84)
  blocking collectives: 171 us -> 78.1 us
  Pallas kernels: 0 us -> 89.9 us
  waiting for transfers between devices: 108 us -> 64 us
  matrix products: 14.7 us -> 7.66 us
    all_to_all x1 -> x0, blocking collectives: 92.4 us -> none  [body(): lax.all_to_all(value, 'group', split_axis=0, concat_axis=0, tiled=True)]
    pallas_call x0 -> x1, Pallas kernels: none -> 89.9 us  [expert_terms(): pl.pallas_call(functools.partial(expert_kernel, groups, chunk), out_shape...]
    all_gather x1 -> x0, waiting for transfers between devices: 41.1 us -> none  [body(): hidden_all = lax.all_gather(hidden, 'group', axis=0, tiled=True)]
    dot_general x2 -> x0, matrix products: 8.39 us -> none  [the longest x1 4.66 us: body(): jnp.dot(picked, both_new, preferred_element_type=jnp.float32)]
    all_gather x1, waiting for transfers between devices: 16.3 us -> 10.5 us  [body(): every = lax.all_gather(mine, 'tp', axis=1, tiled=True)]
  transfers between devices with their start and end apart: 3 -> 2, of which waited for: 3 -> 2; matrix products, arithmetic and copies ran while one was open for 2% -> 4% of each run, Pallas kernels for 0% -> 0%
where the time goes in v2:
time: 270 us; the launch traced here: 269 us
  Pallas kernels  89.9 us (33%)
  blocking collectives  78.1 us (29%)
  waiting for transfers between devices  64 us (24%)
  between operations  13.6 us (5%)
  other arithmetic  8.75 us (3%)
  matrix products  7.66 us (3%)
  local copies, waits for them, and re-layouts  6.94 us (3%)
    pallas_call x1, Pallas kernels, expert_terms(): pl.pallas_call(functools.partial(expert_kernel, groups, chunk), out_shape...  89.9 us
    reduce_scatter x1, waiting for transfers between devices, body(): total = lax.psum_scatter(spread, 'tp', scatter_dimension=0, tiled=True)[0]  53.4 us
    all_to_all x1, blocking collectives, body(): lax.all_to_all(total, 'group', split_axis=0, concat_axis=0, tiled=True)  19.1 us
    all_to_all x1, blocking collectives, body(): lax.all_to_all(mine, 'group', split_axis=0, concat_axis=0, tiled=True)  18.6 us
    all_to_all x1, blocking collectives, body(): mine = lax.all_to_all(tokens, 'tp', split_axis=0, concat_axis=1, tiled=True)  15.1 us
    all_gather x1, blocking collectives, body(): both = lax.all_gather(both, 'group', axis=0, tiled=False)  13.1 us
    all_to_all x1, blocking collectives, body(): lax.all_to_all(total, 'tp', split_axis=1, concat_axis=0, tiled=True)  12.3 us
    all_gather x1, waiting for transfers between devices, body(): every = lax.all_gather(mine, 'tp', axis=1, tiled=True)  10.5 us
  transfers between devices with their start and end apart: 2, of which 2 were waited for; matrix products, arithmetic and copies ran while one was open for 4% of the time, Pallas kernels for 0%

profile of v2, /device:TPU:0, one launch (start us, length us, event | category | flops | bytes accessed | tf_op | source)
XLA Modules:
  0.0 269.0 jit_solution(12377814437417186514)
XLA Ops:
  6.5 0.0 all-gather.4.cloned.1.call-start
  6.6 15.1 %all_to_all.45 = bf16[8,64,512]{2,1,0:T(8,128)(2,1)S(1)} all-to-all(bf16[8,64,512]{2,1,0:T(8,128)(2,1)} %bitcast.58), channel_id=1, replica_groups=mesh['group'=4,'tp'=8] {'tp'}, dimensions={0} | all-to-all | bytes 1048576 | tf_op jit(solution)/shard_map/all_to_all | solution.py:231
  21.7 0.3 copy.25
  21.9 0.3 reshape.85
  22.3 0.2 copy.41
  22.5 18.6 %all_to_all.46 = bf16[4,64,1024]{2,1,0:T(8,128)(2,1)} all-to-all(bf16[4,64,1024]{2,1,0:T(8,128)(2,1)S(1)} %bitcast.54), channel_id=1, replica_groups=mesh['group'=4,'tp'=8] {'group'}, dimensions={0} | all-to-all | bytes 1048576 | tf_op jit(solution)/shard_map/all_to_all | solution.py:233
  41.1 0.0 reduce-scatter.2.cloned.1.call-start
  41.2 0.3 reduce-window.9
  41.5 0.1 slice.13
  41.6 0.1 slice_reduce_fusion
  41.8 0.1 add_add_fusion
  41.9 13.1 %all-gather.1 = f32[4,2,512]{2,1,0:T(2,128)S(1)} all-gather(f32[1,2,512]{2,1,0:T(2,128)S(1)} %maximum_bitcast_fusion), channel_id=2, replica_groups=mesh['group'=4,'tp'=8] {'group'}, dimensions={0}, use_global_device_ids=true | all-gather | bytes 20480 | tf_op jit(solution)/shard_map/all_gather | solution.py:243
  55.1 0.1 copy.27
  55.2 0.4 select_reduce_fusion
  55.6 0.5 reshape.95.weight_ref
  56.1 3.3 %fusion.3 = (bf16[1024,768]{1,0:T(8,128)(2,1)S(1)}, bf16[1024,768]{1,0:T(8,128)(2,1)S(1)}) fusion(bf16[1024,768]{1,0:T(8,128)(2,1)S(1)} %copy-done, f32[8,768]{1,0:T(8,128)S(1)} %convert_element_type.68, bf16[4096,768]{1,0:T(8,128)(2,1)} %param.16, s32[]{:T(128)S(6)} %select_n.32, f32[8,768]{1,0:T(8,128)S(1)} %convert_element_type.64, ...), kind=kLoop, calls=%fused_computation.7 | loop fusion | flops 7864320 | bytes 9486340 | tf_op jit(solution)/shard_map/convert_element_type | solution.py:196
  59.5 2.0 pad_maximum_fusion.w_ref
  61.4 0.9 mul.45
  62.3 0.6 copy-done.1
  62.9 2.6 fusion.1.down_ref
  65.4 10.5 %all-gather.4.cloned.1.call-done = bf16[4,512,1024]{2,1,0:T(8,128)(2,1)} async-done(((bf16[4,64,1024]{2,1,0:T(8,128)(2,1)}), bf16[4,512,1024]{2,1,0:T(8,128)(2,1)}) %all-gather.4.cloned.1.call-update) | async-done | bytes 4194320 | tf_op jit(solution)/shard_map/all_gather | solution.py:234
  75.9 5.3 %fusion.7 = bf16[4,320,1024]{2,1,0:T(8,128)(2,1)} fusion(bf16[4,512,1024]{2,1,0:T(8,128)(2,1)} %all-gather.4.cloned.1.call-done, s32[4,512]{1,0:T(4,128)S(1)} %bitcast.61), kind=kOutput, calls=%fused_computation.14 | convolution fusion | flops 1342832640 | bytes 6823936 | tf_op jit(solution)/shard_map/gsn,gnk->gsk/dot_general | solution.py:249
  81.2 89.9 %shard_map.118 = bf16[1280,1024]{1,0:T(8,128)(2,1)S(1)} custom-call(bf16[1280,1024]{1,0:T(8,128)(2,1)} %bitcast.53, bf16[1024,1536]{1,0:T(8,128)(2,1)} %pad_maximum_fusion.w_ref, bf16[768,1024]{1,0:T(8,128)(2,1)S(1)} %fusion.1.down_ref, f32[1280,1]{1,0:T(8,128)S(1)} %reshape.95.weight_ref), custom_call_target="tpu_custom_call" | custom-call | tf_op jit(solution)/shard_map/pallas_call | solution.py:174
  171.1 2.4 fusion.6
  173.5 2.4 copy.40
  175.9 53.4 %reduce-scatter.2.cloned.1.call-done = bf16[1,4,64,1024]{3,2,1,0:T(8,128)(2,1)} async-done(((bf16[8,4,64,1024]{3,2,1,0:T(8,128)(2,1)}), bf16[1,4,64,1024]{3,2,1,0:T(8,128)(2,1)}) %reduce-scatter.2.cloned.1.call-update) | async-done | bytes 524304 | tf_op jit(solution)/shard_map/reduce_scatter | solution.py:266
  229.3 19.1 %all_to_all.47 = bf16[4,64,1024]{2,1,0:T(8,128)(2,1)S(1)} all-to-all(bf16[4,64,1024]{2,1,0:T(8,128)(2,1)} %bitcast.59), channel_id=1, replica_groups=mesh['group'=4,'tp'=8] {'group'}, dimensions={0} | all-to-all | bytes 1048576 | tf_op jit(solution)/shard_map/all_to_all | solution.py:267
  248.4 0.4 copy.30
  248.8 0.1 all_to_all.37
  249.0 0.2 copy.31
  249.1 12.3 %all_to_all.48 = bf16[64,8,512]{2,0,1:T(8,128)(2,1)S(1)} all-to-all(bf16[64,8,512]{2,0,1:T(8,128)(2,1)S(1)} %copy.31), channel_id=1, replica_groups=mesh['group'=4,'tp'=8] {'tp'}, dimensions={1} | all-to-all | bytes 1048576 | tf_op jit(solution)/shard_map/all_to_all | solution.py:269
  261.4 0.8 copy.45
  (27 shorter events, 0.2 us)
Async XLA Ops:
  6.5 34.6 %copy-start.2 = (s32[512,2]{0,1:T(2,128)S(1)}, s32[512,2]{0,1:T(2,128)}, u32[]{:S(2)}) copy-start(s32[512,2]{0,1:T(2,128)} %param.13) | copy-start | bytes 12292
  6.5 35.1 %copy-start.3 = (f32[512,2]{0,1:T(2,128)S(1)}, f32[512,2]{0,1:T(2,128)}, u32[]{:S(2)}) copy-start(f32[512,2]{0,1:T(2,128)} %param.14) | copy-start | bytes 12292
  6.5 48.5 %copy-start.5 = (bf16[8,768]{1,0:T(8,128)(2,1)S(1)}, bf16[8,768]{1,0:T(8,128)(2,1)}, u32[]{:S(2)}) copy-start(bf16[8,768]{1,0:T(8,128)(2,1)} %param.21) | copy-start | bytes 36868
  6.5 48.5 %copy-start.6 = (bf16[8,768]{1,0:T(8,128)(2,1)S(1)}, bf16[8,768]{1,0:T(8,128)(2,1)}, u32[]{:S(2)}) copy-start(bf16[8,768]{1,0:T(8,128)(2,1)} %param.20) | copy-start | bytes 36868
  6.5 48.5 %copy-start.4 = (bf16[768,8]{0,1:T(8,128)(2,1)S(1)}, bf16[768,8]{0,1:T(8,128)(2,1)}, u32[]{:S(2)}) copy-start(bf16[768,8]{0,1:T(8,128)(2,1)} %param.23) | copy-start | bytes 36868
  6.5 69.4 %all-gather.4.cloned.1.call-start = ((), (), s32[]{:S(2)}) async-start(), calls=%async_computation.5 | async-start | bytes 4718592 | tf_op jit(solution)/shard_map/all_gather | solution.py:234
  21.6 34.5 %copy-start = (bf16[1024,768]{1,0:T(8,128)(2,1)S(1)}, bf16[1024,768]{1,0:T(8,128)(2,1)}, u32[]{:S(2)}) copy-start(bf16[1024,768]{1,0:T(8,128)(2,1)} %param.19) | copy-start | bytes 4718596
  41.1 188.3 %reduce-scatter.2.cloned.1.call-start = ((), (), s32[]{:S(2)}) async-start(), calls=%async_computation.6 | async-start | bytes 4718592 | tf_op jit(solution)/shard_map/reduce_scatter | solution.py:266
  61.4 1.4 copy-start.1
Sparse Core Ops, SparseCore 0:
  41.2 34.6 all-gather.3
  176.0 53.2 reduce-scatter.1

commit v3 on v2

--- a/solution.py
+++ b/solution.py
@@ -203,6 +203,182 @@
         * scale.astype(jnp.float32)[:, :, None]
     )
     return (weight.astype(jnp.float32) + delta.reshape(weight.shape)).astype(jnp.bfloat16)
+
+
+MESH = pl.DeviceIdType.MESH
+
+
+def greet(groups, share, me, mine):
+    barrier = pltpu.get_barrier_semaphore()
+    for d in range(1, groups):
+        where = lax.rem(me + d, groups)
+        pl.semaphore_signal(barrier, inc=1, device_id={"group": where}, device_id_type=MESH)
+    for e in range(1, share):
+        where = lax.rem(mine + e, share)
+        pl.semaphore_signal(barrier, inc=1, device_id={"tp": where}, device_id_type=MESH)
+    pl.semaphore_wait(barrier, groups + share - 2)
+
+
+def total_kernel(groups, share, bits, x_ref, out_ref, *scratch):
+    me, mine = lax.axis_index("group"), lax.axis_index("tp")
+    got = [scratch[2 * i : 2 * i + 2] for i in range(bits)]
+    kept = [scratch[2 * (bits + i) : 2 * (bits + i) + 2] for i in range(bits - 1)]
+    total, gathered, landed, sem, group_sem, plane_sem = scratch[2 * (2 * bits - 1) :]
+    rows, columns = x_ref.shape[-2:]
+    lane = columns // 2
+    orders = [list(range(bits)), [0] + list(range(bits - 1, 0, -1))]
+    part = out_ref.shape[1]
+    ratio = columns // part
+
+    greet(groups, share, me, mine)
+
+    def digit(b):
+        return lax.rem(mine // (1 << b), 2)
+
+    def source(i, p, g, own):
+        b = orders[p][i]
+        left = sorted(set(range(bits)) - set(orders[p][:i]), reverse=True)
+        wanted = digit(b) if own else 1 - digit(b)
+        index = [g] + [wanted if other == b else slice(None) for other in left]
+        if i == 0:
+            return x_ref.at[tuple(index + [slice(None), pl.ds(p * lane, lane)])]
+        return kept[i - 1][p].at[tuple(index)]
+
+    def halving(i, p, g):
+        b = orders[p][i]
+        partner = mine + (1 << b) * (1 - 2 * digit(b))
+        return pltpu.make_async_remote_copy(
+            src_ref=source(i, p, g, False),
+            dst_ref=got[i][p].at[g],
+            send_sem=sem.at[0, i, p, g],
+            recv_sem=sem.at[1, i, p, g],
+            device_id={"tp": partner},
+            device_id_type=MESH,
+        )
+
+    for g in range(groups):
+        for p in range(2):
+            halving(0, p, g).start()
+    for i in range(bits):
+        for g in range(groups):
+            for p in range(2):
+                halving(i, p, g).wait_recv()
+                value = source(i, p, g, True)[...].astype(jnp.float32)
+                value = (value + got[i][p][g].astype(jnp.float32)).astype(jnp.bfloat16)
+                if i < bits - 1:
+                    kept[i][p][g] = value
+                    halving(i + 1, p, g).start()
+                else:
+                    total[g, :, p * lane : (p + 1) * lane] = value
+
+    def to_group(d):
+        where = lax.rem(me + d, groups)
+        return pltpu.make_async_remote_copy(
+            src_ref=total.at[where],
+            dst_ref=gathered.at[me],
+            send_sem=group_sem.at[0, d],
+            recv_sem=group_sem.at[1, d],
+            device_id={"group": where},
+            device_id_type=MESH,
+        )
+
+    def from_group(d):
+        where = lax.rem(me + groups - d, groups)
+        return pltpu.make_async_remote_copy(
+            src_ref=total.at[where],
+            dst_ref=gathered.at[where],
+            send_sem=group_sem.at[0, d],
+            recv_sem=group_sem.at[1, d],
+            device_id={"group": where},
+            device_id_type=MESH,
+        )
+
+    def to_columns(where, slot, offset):
+        return pltpu.make_async_remote_copy(
+            src_ref=gathered.at[slot, :, pl.ds(offset, part)],
+            dst_ref=landed.at[pl.ds(pl.multiple_of(mine * rows, rows), rows)],
+            send_sem=plane_sem.at[0, where],
+            recv_sem=plane_sem.at[1, mine],
+            device_id={"tp": where},
+            device_id_type=MESH,
+        )
+
+    for d in range(1, groups):
+        to_group(d).start()
+    gathered[me] = total[me]
+    for d in range(groups):
+        slot = lax.rem(me + groups - d, groups)
+        if d > 0:
+            from_group(d).wait_recv()
+        for r in range(ratio):
+            where = slot * ratio + r
+
+            @pl.when(where != mine)
+            def _():
+                to_columns(where, slot, r * part).start()
+
+            @pl.when(where == mine)
+            def _():
+                landed[pl.ds(pl.multiple_of(mine * rows, rows), rows), :] = gathered[
+                    slot, :, r * part : (r + 1) * part
+                ]
+
+    def passed(where):
+        return pltpu.make_async_remote_copy(
+            src_ref=gathered.at[0, :, pl.ds(0, part)],
+            dst_ref=landed.at[pl.ds(pl.multiple_of(where * rows, rows), rows)],
+            send_sem=plane_sem.at[0, where],
+            recv_sem=plane_sem.at[1, where],
+            device_id={"tp": where},
+            device_id_type=MESH,
+        )
+
+    for e in range(1, share):
+        passed(lax.rem(mine + e, share)).wait_recv()
+    out_ref[...] = landed[...]
+    for e in range(1, share):
+        where = lax.rem(mine + e, share)
+        slot = where // ratio
+        for r in range(ratio):
+
+            @pl.when(lax.rem(where, ratio) == r)
+            def _():
+                to_columns(where, slot, r * part).wait_send()
+
+    for d in range(1, groups):
+        to_group(d).wait_send()
+    for i in range(bits):
+        for g in range(groups):
+            for p in range(2):
+                halving(i, p, g).wait_send()
+
+
+def total_rows(groups, share, spread, part):
+    rows, columns = spread.shape[1], spread.shape[2]
+    bits = share.bit_length() - 1
+    block = rows // share
+    vmem = pl.BlockSpec(memory_space=pltpu.VMEM)
+    sizes = [(groups,) + (2,) * (bits - 1 - i) + (block, columns // 2) for i in range(bits)]
+    buffers = [pltpu.VMEM(size, jnp.bfloat16) for size in sizes for _ in range(2)]
+    return pl.pallas_call(
+        functools.partial(total_kernel, groups, share, bits),
+        out_shape=jax.ShapeDtypeStruct((rows, part), jnp.bfloat16),
+        in_specs=[vmem],
+        out_specs=vmem,
+        scratch_shapes=[
+            *buffers,
+            *buffers[:-2],
+            pltpu.VMEM((groups, block, columns), jnp.bfloat16),
+            pltpu.VMEM((groups, block, columns), jnp.bfloat16),
+            pltpu.VMEM((rows, part), jnp.bfloat16),
+            pltpu.SemaphoreType.DMA((2, bits, 2, groups)),
+            pltpu.SemaphoreType.DMA((2, groups)),
+            pltpu.SemaphoreType.DMA((2, share)),
+        ],
+        compiler_params=pltpu.CompilerParams(
+            collective_id=1, has_side_effects=True, vmem_limit_bytes=48 * 1024 * 1024
+        ),
+    )(spread.reshape((groups,) + (2,) * bits + (block, columns)))
 
 
 def body(
@@ -262,11 +438,7 @@
     term = expert_terms(groups, picked, both_new, down_new, slot_weight.reshape(-1, 1))
     term = term.reshape(groups, capacity, columns)
     spread = jnp.einsum("gsn,gsk->gnk", pick, term)
-    spread = spread.reshape(groups, share, rows // share, columns).transpose(1, 0, 2, 3)
-    total = lax.psum_scatter(spread, "tp", scatter_dimension=0, tiled=True)[0]
-    total = lax.all_to_all(total, "group", split_axis=0, concat_axis=0, tiled=True)
-    total = total.transpose(1, 0, 2).reshape(rows // share, width)
-    return lax.all_to_all(total, "tp", split_axis=1, concat_axis=0, tiled=True).astype(jnp.bfloat16)
+    return total_rows(groups, share, spread, part)
 
 
 def solution(mesh):

time: 270 us -> 224 us (0.83)
  waiting for transfers between devices: 64 us -> 10.6 us
  Pallas kernels: 89.9 us -> 131 us
  blocking collectives: 78.1 us -> 46.8 us
  local copies, waits for them, and re-layouts: 6.94 us -> 3.93 us
    reduce_scatter x1 -> x0, waiting for transfers between devices: 53.4 us -> none  [body(): total = lax.psum_scatter(spread, 'tp', scatter_dimension=0, tiled=True)[0]]
    pallas_call x0 -> x1, Pallas kernels: none -> 40.9 us  [total_rows(): pl.pallas_call(functools.partial(total_kernel, groups, share, bits), out_...]
    all_to_all x2 -> x0, blocking collectives: 31.4 us -> none  [the longest x1 19.1 us: body(): lax.all_to_all(total, 'group', split_axis=0, concat_axis=0, tiled=True)]
  transfers between devices with their start and end apart: 2 -> 1, of which waited for: 2 -> 1; matrix products, arithmetic and copies ran while one was open for 4% -> 5% of each run, Pallas kernels for 0% -> 0%
where the time goes in v3:
time: 224 us; the launch traced here: 222 us
  Pallas kernels  131 us (58%)
  blocking collectives  46.8 us (21%)
  between operations  13.6 us (6%)
  waiting for transfers between devices  10.6 us (5%)
  other arithmetic  8.71 us (4%)
  matrix products  7.66 us (3%)
  local copies, waits for them, and re-layouts  3.93 us (2%)
    pallas_call x1, Pallas kernels, expert_terms(): pl.pallas_call(functools.partial(expert_kernel, groups, chunk), out_shape...  89.9 us
    pallas_call x1, Pallas kernels, total_rows(): pl.pallas_call(functools.partial(total_kernel, groups, share, bits), out_...  40.9 us
    all_to_all x1, blocking collectives, body(): lax.all_to_all(mine, 'group', split_axis=0, concat_axis=0, tiled=True)  18.6 us
    all_to_all x1, blocking collectives, body(): mine = lax.all_to_all(tokens, 'tp', split_axis=0, concat_axis=1, tiled=True)  15.1 us
    all_gather x1, blocking collectives, body(): both = lax.all_gather(both, 'group', axis=0, tiled=False)  13.1 us
    all_gather x1, waiting for transfers between devices, body(): every = lax.all_gather(mine, 'tp', axis=1, tiled=True)  10.5 us
    dot_general x1, matrix products, body(): picked = jnp.einsum('gsn,gnk->gsk', pick, every)  5.28 us
  transfers between devices with their start and end apart: 1, of which 1 were waited for; matrix products, arithmetic and copies ran while one was open for 5% of the time, Pallas kernels for 0%

profile of v3, /device:TPU:0, one launch (start us, length us, event | category | flops | bytes accessed | tf_op | source)
XLA Modules:
  0.0 222.1 jit_solution(2512401414762956795)
XLA Ops:
  6.5 0.0 all-gather.4.cloned.1.call-start
  6.6 15.1 %all_to_all.21 = bf16[8,64,512]{2,1,0:T(8,128)(2,1)S(1)} all-to-all(bf16[8,64,512]{2,1,0:T(8,128)(2,1)} %bitcast.47), channel_id=1, replica_groups=mesh['group'=4,'tp'=8] {'tp'}, dimensions={0} | all-to-all | bytes 1048576 | tf_op jit(solution)/shard_map/all_to_all | solution.py:407
  21.7 0.3 copy.18
  21.9 0.3 reshape.80
  22.3 0.2 copy.29
  22.5 18.6 %all_to_all.22 = bf16[4,64,1024]{2,1,0:T(8,128)(2,1)} all-to-all(bf16[4,64,1024]{2,1,0:T(8,128)(2,1)S(1)} %bitcast.45), channel_id=1, replica_groups=mesh['group'=4,'tp'=8] {'group'}, dimensions={0} | all-to-all | bytes 1048576 | tf_op jit(solution)/shard_map/all_to_all | solution.py:409
  41.1 0.0 all-gather.4.cloned.1.call-update
  41.1 0.0 copy-done.2
  41.2 0.3 reduce-window.9
  41.5 0.1 slice.13
  41.6 0.0 copy-done.3
  41.6 0.1 slice_reduce_fusion
  41.7 0.1 add_add_fusion
  41.8 13.1 %all-gather.1 = f32[4,2,512]{2,1,0:T(2,128)S(1)} all-gather(f32[1,2,512]{2,1,0:T(2,128)S(1)} %maximum_bitcast_fusion), channel_id=2, replica_groups=mesh['group'=4,'tp'=8] {'group'}, dimensions={0}, use_global_device_ids=true | all-gather | bytes 20480 | tf_op jit(solution)/shard_map/all_gather | solution.py:419
  55.0 0.0 copy-done.5
  55.0 0.0 copy-done.6
  55.0 0.0 copy-done.4
  55.0 0.1 copy.20
  55.2 0.4 select_reduce_fusion
  55.6 0.5 reshape.90.weight_ref
  56.1 0.0 copy-done
  56.1 3.3 %fusion.3 = (bf16[1024,768]{1,0:T(8,128)(2,1)S(1)}, bf16[1024,768]{1,0:T(8,128)(2,1)S(1)}) fusion(bf16[1024,768]{1,0:T(8,128)(2,1)S(1)} %copy-done, f32[8,768]{1,0:T(8,128)S(1)} %convert_element_type.68, bf16[4096,768]{1,0:T(8,128)(2,1)} %param.16, s32[]{:T(128)S(6)} %select_n.32, f32[8,768]{1,0:T(8,128)S(1)} %convert_element_type.64, ...), kind=kLoop, calls=%fused_computation.6 | loop fusion | flops 7864320 | bytes 9486340 | tf_op jit(solution)/shard_map/convert_element_type | solution.py:196
  59.4 1.9 pad_maximum_fusion.w_ref
  61.3 0.9 mul.45
  62.2 0.6 copy-done.1
  62.8 2.6 %fusion.1.down_ref = bf16[768,1024]{1,0:T(8,128)(2,1)S(1)} fusion(f32[96,8,8,128]{3,2,1,0:T(8,128)S(1)} %bitcast.43, bf16[768,1024]{1,0:T(8,128)(2,1)S(1)} %copy-done.1, bf16[768,4096]{1,0:T(8,128)(2,1)} %param.17, s32[]{:T(128)S(6)} %select_n.32), kind=kLoop, calls=%fused_computation.2 | loop fusion | flops 3932160 | bytes 7864324 | tf_op jit(solution)/shard_map/convert_element_type | solution.py:205
  65.4 10.5 %all-gather.4.cloned.1.call-done = bf16[4,512,1024]{2,1,0:T(8,128)(2,1)} async-done(((bf16[4,64,1024]{2,1,0:T(8,128)(2,1)}), bf16[4,512,1024]{2,1,0:T(8,128)(2,1)}) %all-gather.4.cloned.1.call-update) | async-done | bytes 4194320 | tf_op jit(solution)/shard_map/all_gather | solution.py:410
  75.9 5.3 %fusion.7 = bf16[4,320,1024]{2,1,0:T(8,128)(2,1)} fusion(bf16[4,512,1024]{2,1,0:T(8,128)(2,1)} %all-gather.4.cloned.1.call-done, s32[4,512]{1,0:T(4,128)S(1)} %bitcast.49), kind=kOutput, calls=%fused_computation.13 | convolution fusion | flops 1342832640 | bytes 6823936 | tf_op jit(solution)/shard_map/gsn,gnk->gsk/dot_general | solution.py:425
  81.2 89.9 %shard_map.118 = bf16[1280,1024]{1,0:T(8,128)(2,1)S(1)} custom-call(bf16[1280,1024]{1,0:T(8,128)(2,1)} %bitcast.44, bf16[1024,1536]{1,0:T(8,128)(2,1)} %pad_maximum_fusion.w_ref, bf16[768,1024]{1,0:T(8,128)(2,1)S(1)} %fusion.1.down_ref, f32[1280,1]{1,0:T(8,128)S(1)} %reshape.90.weight_ref), custom_call_target="tpu_custom_call" | custom-call | tf_op jit(solution)/shard_map/pallas_call | solution.py:174
  171.1 2.4 %fusion.6 = bf16[4,512,1024]{2,1,0:T(8,128)(2,1)S(1)} fusion(bf16[4,320,1024]{2,1,0:T(8,128)(2,1)S(1)} %bitcast.42, s32[4,512]{1,0:T(4,128)S(1)} %bitcast.50), kind=kOutput, calls=%fused_computation.12 | convolution fusion | flops 1342832640 | bytes 6823936 | tf_op jit(solution)/shard_map/gsn,gsk->gnk/dot_general | solution.py:440
  173.5 40.9 %shard_map.119 = bf16[512,512]{1,0:T(8,128)(2,1)S(1)} custom-call(bf16[4,2,2,2,64,1024]{5,4,3,2,1,0:T(8,128)(2,1)S(1)} %bitcast.41), custom_call_target="tpu_custom_call" | custom-call | tf_op jit(solution)/shard_map/pallas_call | solution.py:363
  214.4 0.8 copy.33
  (19 shorter events, 0.2 us)
Async XLA Ops:
  6.5 34.6 %copy-start.2 = (s32[512,2]{0,1:T(2,128)S(1)}, s32[512,2]{0,1:T(2,128)}, u32[]{:S(2)}) copy-start(s32[512,2]{0,1:T(2,128)} %param.13) | copy-start | bytes 12292
  6.5 35.0 %copy-start.3 = (f32[512,2]{0,1:T(2,128)S(1)}, f32[512,2]{0,1:T(2,128)}, u32[]{:S(2)}) copy-start(f32[512,2]{0,1:T(2,128)} %param.14) | copy-start | bytes 12292
  6.5 48.5 %copy-start.5 = (bf16[8,768]{1,0:T(8,128)(2,1)S(1)}, bf16[8,768]{1,0:T(8,128)(2,1)}, u32[]{:S(2)}) copy-start(bf16[8,768]{1,0:T(8,128)(2,1)} %param.21) | copy-start | bytes 36868
  6.5 48.5 %copy-start.6 = (bf16[8,768]{1,0:T(8,128)(2,1)S(1)}, bf16[8,768]{1,0:T(8,128)(2,1)}, u32[]{:S(2)}) copy-start(bf16[8,768]{1,0:T(8,128)(2,1)} %param.20) | copy-start | bytes 36868
  6.5 48.5 %copy-start.4 = (bf16[768,8]{0,1:T(8,128)(2,1)S(1)}, bf16[768,8]{0,1:T(8,128)(2,1)}, u32[]{:S(2)}) copy-start(bf16[768,8]{0,1:T(8,128)(2,1)} %param.23) | copy-start | bytes 36868
  6.5 69.4 %all-gather.4.cloned.1.call-start = ((), (), s32[]{:S(2)}) async-start(), calls=%async_computation.2 | async-start | bytes 4718592 | tf_op jit(solution)/shard_map/all_gather | solution.py:410
  21.6 34.4 %copy-start = (bf16[1024,768]{1,0:T(8,128)(2,1)S(1)}, bf16[1024,768]{1,0:T(8,128)(2,1)}, u32[]{:S(2)}) copy-start(bf16[1024,768]{1,0:T(8,128)(2,1)} %param.19) | copy-start | bytes 4718596
  61.3 1.5 copy-start.1
Sparse Core Ops, SparseCore 0:
  41.2 34.6 all-gather.3

commit v4 on v3

--- a/solution.py
+++ b/solution.py
@@ -381,6 +381,199 @@
     )(spread.reshape((groups,) + (2,) * bits + (block, columns)))
 
 
+def pick_kernel(
+    groups,
+    share,
+    bits,
+    tokens_ref,
+    route_ref,
+    picked_ref,
+    pick_ref,
+    weight_ref,
+    mid,
+    every,
+    table,
+    table_sem,
+    plane_sem,
+    group_sem,
+    sem,
+):
+    me, mine = lax.axis_index("group"), lax.axis_index("tp")
+    rows, columns = mid.shape[1:]
+    part = tokens_ref.shape[1]
+    ratio = columns // part
+    lane = columns // 2
+    capacity = picked_ref.shape[1]
+    orders = [list(range(bits - 1, -1, -1)), list(range(1, bits)) + [0]]
+
+    greet(groups, share, me, mine)
+
+    def digit(b):
+        return lax.rem(mine // (1 << b), 2)
+
+    def route(d, sending):
+        slot = me if sending else lax.rem(me + groups - d, groups)
+        where = lax.rem(me + d, groups)
+        return pltpu.make_async_remote_copy(
+            src_ref=route_ref,
+            dst_ref=table.at[slot],
+            send_sem=table_sem.at[0, d],
+            recv_sem=table_sem.at[1, d],
+            device_id={"group": where},
+            device_id_type=MESH,
+        )
+
+    def block(where, slot, r, source):
+        return pltpu.make_async_remote_copy(
+            src_ref=tokens_ref.at[pl.ds(pl.multiple_of(where * rows, rows), rows)],
+            dst_ref=mid.at[slot, :, pl.ds(r * part, part)],
+            send_sem=plane_sem.at[0, where],
+            recv_sem=plane_sem.at[1, source],
+            device_id={"tp": where},
+            device_id_type=MESH,
+        )
+
+    place = [digit(b) for b in range(bits - 1, -1, -1)]
+
+    def slice_move(d, sending):
+        where = lax.rem(me + d, groups)
+        slot = me if sending else lax.rem(me + groups - d, groups)
+        return pltpu.make_async_remote_copy(
+            src_ref=mid.at[where],
+            dst_ref=every.at[tuple([slot] + place)],
+            send_sem=group_sem.at[0, d],
+            recv_sem=group_sem.at[1, d],
+            device_id={"group": where},
+            device_id_type=MESH,
+        )
+
+    def doubling(i, p, d, sending):
+        b = orders[p][i]
+        done = orders[p][:i]
+        slot = lax.rem(me + groups - d, groups)
+        index = [slot]
+        for other in range(bits - 1, -1, -1):
+            if other in done:
+                index.append(slice(None))
+            elif other == b and not sending:
+                index.append(1 - digit(other))
+            else:
+                index.append(digit(other))
+        view = every.at[tuple(index + [slice(None), pl.ds(p * lane, lane)])]
+        return pltpu.make_async_remote_copy(
+            src_ref=view,
+            dst_ref=view,
+            send_sem=sem.at[0, i, p, d],
+            recv_sem=sem.at[1, i, p, d],
+            device_id={"tp": mine + (1 << b) * (1 - 2 * digit(b))},
+            device_id_type=MESH,
+        )
+
+    def blocks(e, act):
+        where = lax.rem(mine + e, share)
+        for r in range(ratio):
+
+            @pl.when(lax.rem(mine, ratio) == r)
+            def _():
+                act(block(where, mine // ratio, r, mine))
+
+    for e in range(1, share):
+        blocks(e, lambda copy: copy.start())
+    for d in range(1, groups):
+        route(d, True).start()
+    for r in range(ratio):
+
+        @pl.when(lax.rem(mine, ratio) == r)
+        def _():
+            mid[mine // ratio, :, r * part : (r + 1) * part] = tokens_ref[
+                pl.ds(pl.multiple_of(mine * rows, rows), rows), :
+            ]
+
+    table[me] = route_ref[...]
+    for d in list(range(1, groups)) + [0]:
+        slot = lax.rem(me + d, groups)
+        for r in range(ratio):
+            origin = slot * ratio + r
+
+            @pl.when(origin != mine)
+            def _():
+                block(origin, slot, r, origin).wait_recv()
+
+        if d > 0:
+            slice_move(d, True).start()
+        else:
+            every[tuple([me] + place)] = mid[me]
+
+    for d in range(groups):
+        if d > 0:
+            slice_move(d, False).wait_recv()
+        for p in range(2):
+            doubling(0, p, d, True).start()
+    for i in range(bits):
+        for d in range(groups):
+            for p in range(2):
+                doubling(i, p, d, False).wait_recv()
+                if i < bits - 1:
+                    doubling(i + 1, p, d, True).start()
+            if i == bits - 1:
+                slot = lax.rem(me + groups - d, groups)
+                if d > 0:
+                    route(d, False).wait_recv()
+                entry = table[slot]
+                number = lax.broadcasted_iota(jnp.int32, (capacity, entry.shape[1]), 0)
+                chosen = number.astype(jnp.float32) == entry[0:1, :]
+                weight_ref[slot] = jnp.sum(
+                    jnp.where(chosen, entry[1:2, :], 0.0), axis=1, keepdims=True
+                )
+                chosen = jnp.where(chosen, 1.0, 0.0).astype(jnp.bfloat16)
+                pick_ref[slot] = chosen
+                picked_ref[slot] = jnp.dot(
+                    chosen,
+                    every[slot].reshape(share * rows, columns),
+                    preferred_element_type=jnp.float32,
+                ).astype(jnp.bfloat16)
+
+    for e in range(1, share):
+        blocks(e, lambda copy: copy.wait_send())
+    for d in range(1, groups):
+        route(d, True).wait_send()
+        slice_move(d, True).wait_send()
+    for i in range(bits):
+        for d in range(groups):
+            for p in range(2):
+                doubling(i, p, d, True).wait_send()
+
+
+def pick_rows(groups, share, tokens, route, capacity):
+    rows, part = tokens.shape
+    columns = part * share // groups
+    bits = share.bit_length() - 1
+    block = rows // share
+    vmem = pl.BlockSpec(memory_space=pltpu.VMEM)
+    return pl.pallas_call(
+        functools.partial(pick_kernel, groups, share, bits),
+        out_shape=(
+            jax.ShapeDtypeStruct((groups, capacity, columns), jnp.bfloat16),
+            jax.ShapeDtypeStruct((groups, capacity, rows), jnp.bfloat16),
+            jax.ShapeDtypeStruct((groups, capacity, 1), jnp.float32),
+        ),
+        in_specs=[vmem] * 2,
+        out_specs=(vmem,) * 3,
+        scratch_shapes=[
+            pltpu.VMEM((groups, block, columns), jnp.bfloat16),
+            pltpu.VMEM((groups,) + (2,) * bits + (block, columns), jnp.bfloat16),
+            pltpu.VMEM((groups,) + route.shape, jnp.float32),
+            pltpu.SemaphoreType.DMA((2, groups)),
+            pltpu.SemaphoreType.DMA((2, share)),
+            pltpu.SemaphoreType.DMA((2, groups)),
+            pltpu.SemaphoreType.DMA((2, bits, 2, groups)),
+        ],
+        compiler_params=pltpu.CompilerParams(
+            collective_id=2, has_side_effects=True, vmem_limit_bytes=48 * 1024 * 1024
+        ),
+    )(tokens, route)
+
+
 def body(
     tokens,
     route_ids,
@@ -404,25 +597,15 @@
     capacity = rows * route_ids.shape[1] * 5 // (EXPERTS * 4)
     expert = lax.axis_index("tp") // (share // EXPERTS)
 
-    mine = lax.all_to_all(tokens, "tp", split_axis=0, concat_axis=1, tiled=True)
-    mine = mine.reshape(rows // share, groups, depth).transpose(1, 0, 2)
-    mine = lax.all_to_all(mine, "group", split_axis=0, concat_axis=0, tiled=True)
-    every = lax.all_gather(mine, "tp", axis=1, tiled=True)
-
     combine = route_weight / jnp.sum(route_weight, axis=1, keepdims=True)
     named = route_ids == expert
     weight_row = jnp.sum(jnp.where(named, combine, jnp.zeros_like(combine)), axis=1)
     used = jnp.any(named, axis=1)
     place = jnp.cumsum(used.astype(jnp.int32)) - 1
     target = jnp.where(used, place, capacity)
-    both = jnp.stack([target.astype(jnp.float32), weight_row], axis=0)
-    both = lax.all_gather(both, "group", axis=0, tiled=False)
-    target_all = both[:, 0].astype(jnp.int32)
-    pick = target_all[:, None, :] == lax.broadcasted_iota(jnp.int32, (groups, capacity, rows), 1)
-    slot_weight = jnp.sum(jnp.where(pick, both[:, 1][:, None, :], 0.0), axis=2)
-    pick = pick.astype(jnp.bfloat16)
-
-    picked = jnp.einsum("gsn,gnk->gsk", pick, every)
+    route = jnp.stack([target.astype(jnp.float32), weight_row], axis=0)
+    route = jnp.pad(route, ((0, 6), (0, 0)))
+    picked, pick, slot_weight = pick_rows(groups, share, tokens, route, capacity)
     picked = picked.reshape(groups * capacity, depth)
 
     gate_new = refresh_rows(

time: 224 us -> 196 us (0.88)
  blocking collectives: 46.8 us -> 0 us
  Pallas kernels: 131 us -> 175 us
  between operations: 13.6 us -> 0.12 us
  waiting for transfers between devices: 10.6 us -> 0 us
  matrix products: 7.66 us -> 2.37 us
  other arithmetic: 8.71 us -> 11.7 us
    pallas_call x0 -> x1, Pallas kernels: none -> 41.9 us  [pick_rows(): pl.pallas_call(functools.partial(pick_kernel, groups, share, bits), out_s...]
    all_to_all x2 -> x0, blocking collectives: 33.7 us -> none  [the longest x1 18.6 us: body(): lax.all_to_all(mine, 'group', split_axis=0, concat_axis=0, tiled=True)]
    all_gather x1 -> x0, blocking collectives: 13.1 us -> none  [body(): both = lax.all_gather(both, 'group', axis=0, tiled=False)]
    all_gather x1 -> x0, waiting for transfers between devices: 10.5 us -> none  [body(): every = lax.all_gather(mine, 'tp', axis=1, tiled=True)]
    dot_general x1 -> x0, matrix products: 5.28 us -> none  [body(): picked = jnp.einsum('gsn,gnk->gsk', pick, every)]
    pallas_call x1, Pallas kernels: 89.9 us -> 92.3 us  [expert_terms(): pl.pallas_call(functools.partial(expert_kernel, groups, chunk), out_shape...]
  transfers between devices with their start and end apart: 1 -> 0, of which waited for: 1 -> 0; matrix products, arithmetic and copies ran while one was open for 5% -> 0% of each run, Pallas kernels for 0% -> 0%
where the time goes in v4:
time: 196 us; the launch traced here: 193 us
  Pallas kernels  175 us (89%)
  other arithmetic  11.7 us (6%)
  local copies, waits for them, and re-layouts  4.24 us (2%)
  matrix products  2.37 us (1%)
    pallas_call x1, Pallas kernels, expert_terms(): pl.pallas_call(functools.partial(expert_kernel, groups, chunk), out_shape...  92.3 us
    pallas_call x1, Pallas kernels, pick_rows(): pl.pallas_call(functools.partial(pick_kernel, groups, share, bits), out_s...  41.9 us
    pallas_call x1, Pallas kernels, total_rows(): pl.pallas_call(functools.partial(total_kernel, groups, share, bits), out_...  40.6 us

profile of v4, /device:TPU:0, one launch (start us, length us, event | category | flops | bytes accessed | tf_op | source)
XLA Modules:
  0.0 193.3 jit_solution(13764473528675084374)
XLA Ops:
  0.0 0.0 copy-start.4
  0.0 0.8 fusion.8
  0.8 0.3 reduce-window.9
  1.1 0.1 slice.7
  1.3 0.1 slice_reduce_fusion
  1.4 0.1 add_add_fusion
  1.5 0.7 reduce_sum.18
  2.2 0.7 fusion.6
  2.9 0.7 convert_element_type.60
  3.6 0.7 convert_element_type.64
  4.3 0.8 copy.14
  5.2 0.9 mul.45
  6.0 0.0 copy-done.4
  6.1 0.0 copy-start.2
  6.1 0.0 copy-start.3
  6.1 2.7 %fusion.1.down_ref = bf16[768,1024]{1,0:T(8,128)(2,1)S(1)} fusion(f32[96,8,8,128]{3,2,1,0:T(8,128)S(1)} %bitcast.33, bf16[768,1024]{1,0:T(8,128)(2,1)S(1)} %copy-done.4, bf16[768,4096]{1,0:T(8,128)(2,1)} %param.17, s32[]{:T(128)S(6)} %select_n.28), kind=kLoop, calls=%fused_computation.2 | loop fusion | flops 3932160 | bytes 7864324 | tf_op jit(solution)/shard_map/convert_element_type | solution.py:205
  8.8 0.0 copy-done.2
  8.8 0.0 copy-done.3
  8.9 2.9 %fusion.3 = (bf16[1024,768]{1,0:T(8,128)(2,1)S(1)}, bf16[1024,768]{1,0:T(8,128)(2,1)S(1)}) fusion(bf16[1024,768]{1,0:T(8,128)(2,1)S(1)} %copy-done.2, f32[8,768]{1,0:T(8,128)S(1)} %convert_element_type.64, bf16[4096,768]{1,0:T(8,128)(2,1)} %param.16, s32[]{:T(128)S(6)} %select_n.28, f32[8,768]{1,0:T(8,128)S(1)} %convert_element_type.60, ...), kind=kLoop, calls=%fused_computation.6 | loop fusion | flops 7864320 | bytes 9486340 | tf_op jit(solution)/shard_map/convert_element_type | solution.py:196
  11.8 0.0 copy-start.1
  11.8 1.9 pad_maximum_fusion.w_ref
  13.7 0.0 copy-done.1
  13.7 41.9 %shard_map.118 = (bf16[4,320,1024]{2,1,0:T(8,128)(2,1)S(1)}, bf16[4,320,512]{2,1,0:T(8,128)(2,1)S(1)}, f32[4,320,1]{2,1,0:T(8,128)S(1)}) custom-call(bf16[512,512]{1,0:T(8,128)(2,1)S(1)} %copy-done.1, f32[8,512]{1,0:T(8,128)S(1)} %select_maximum_fusion.route_ref), custom_call_target="tpu_custom_call" | custom-call | tf_op jit(solution)/shard_map/pallas_call | solution.py:553
  55.6 0.0 copy-start
  55.6 1.5 copy-done
  57.1 92.3 %shard_map.119 = bf16[1280,1024]{1,0:T(8,128)(2,1)S(1)} custom-call(bf16[1280,1024]{1,0:T(8,128)(2,1)} %bitcast.31, bf16[1024,1536]{1,0:T(8,128)(2,1)} %pad_maximum_fusion.w_ref, bf16[768,1024]{1,0:T(8,128)(2,1)S(1)} %fusion.1.down_ref, f32[1280,1]{1,0:T(8,128)S(1)} %bitcast.32), custom_call_target="tpu_custom_call" | custom-call | tf_op jit(solution)/shard_map/pallas_call | solution.py:174
  149.5 2.4 %fusion.9 = bf16[4,512,1024]{2,1,0:T(8,128)(2,1)S(1)} fusion(bf16[4,320,512]{2,1,0:T(8,128)(2,1)S(1)} %get-tuple-element.8, bf16[4,320,1024]{2,1,0:T(8,128)(2,1)S(1)} %bitcast.30), kind=kOutput, calls=%fused_computation.21 | convolution fusion | flops 1342177280 | bytes 8126464 | tf_op jit(solution)/shard_map/gsn,gsk->gnk/dot_general | solution.py:623
  151.8 40.6 %shard_map.120 = bf16[512,512]{1,0:T(8,128)(2,1)S(1)} custom-call(bf16[4,2,2,2,64,1024]{5,4,3,2,1,0:T(8,128)(2,1)S(1)} %bitcast.29), custom_call_target="tpu_custom_call" | custom-call | tf_op jit(solution)/shard_map/pallas_call | solution.py:363
  192.5 0.8 copy.18
  (4 shorter events, 0.1 us)
Async XLA Ops:
  0.0 6.0 %copy-start.4 = (bf16[768,1024]{1,0:T(8,128)(2,1)S(1)}, bf16[768,1024]{1,0:T(8,128)(2,1)}, u32[]{:S(2)}) copy-start(bf16[768,1024]{1,0:T(8,128)(2,1)} %param.22) | copy-start | bytes 4718596
  6.1 2.8 %copy-start.2 = (bf16[1024,768]{1,0:T(8,128)(2,1)S(1)}, bf16[1024,768]{1,0:T(8,128)(2,1)}, u32[]{:S(2)}) copy-start(bf16[1024,768]{1,0:T(8,128)(2,1)} %param.19) | copy-start | bytes 4718596
  6.1 2.8 %copy-start.3 = (bf16[1024,768]{1,0:T(8,128)(2,1)S(1)}, bf16[1024,768]{1,0:T(8,128)(2,1)}, u32[]{:S(2)}) copy-start(bf16[1024,768]{1,0:T(8,128)(2,1)} %param.18) | copy-start | bytes 4718596
  11.8 1.9 copy-start.1
  55.6 1.5 copy-start

commit v5 on v4

--- a/solution.py
+++ b/solution.py
@@ -24,6 +24,7 @@
     in_up,
     in_low,
     hidden,
+    ahead,
     sem,
 ):
     me = lax.axis_index("group")
@@ -87,7 +88,7 @@
         first, final = (0, last) if upward else (last, 0)
         inside, outside = (in_up, out_up) if upward else (in_low, out_low)
         here = piece(k, 0)
-        own = jnp.dot(x_ref[piece(k, start), :], w_ref[...], preferred_element_type=jnp.float32)
+        own = ahead[int(upward)]
 
         @pl.when(me == first)
         def _():
@@ -116,7 +117,18 @@
         @pl.when(me == final)
         def _():
             hidden_move(k, upward).start()
-            finish(k, start)
+
+    def prepare(t):
+        for upward in (True, False):
+            k = t - (me if upward else last - me)
+
+            @pl.when((k >= 0) & (k < count))
+            def _():
+                ahead[int(upward)] = jnp.dot(
+                    x_ref[piece(k, half if upward else 0), :],
+                    w_ref[...],
+                    preferred_element_type=jnp.float32,
+                )
 
     def take(k, upward):
         final, end = (last, 0) if upward else (0, last)
@@ -125,8 +137,6 @@
         @pl.when(me != end)
         def _():
             hidden_move(k, upward).start()
-
-        finish(k, half if upward else 0)
 
     def step(t, _):
         for upward in (True, False):
@@ -137,6 +147,17 @@
             def _():
                 add(k, upward)
 
+        prepare(t + 1)
+        for upward in (True, False):
+            place = me if upward else last - me
+            k = t - place
+            j = k - 1 - 2 * (last - place)
+            k = jnp.where(place == last, k, j)
+
+            @pl.when((k >= 0) & (k < count))
+            def _():
+                finish(k, half if upward else 0)
+
         for upward in (True, False):
             place = me if upward else last - me
             j = t - (2 * last - place)
@@ -147,7 +168,8 @@
 
         return 0
 
-    lax.fori_loop(0, count + 2 * last, step, 0)
+    prepare(0)
+    lax.fori_loop(0, count + 2 * last + 1, step, 0)
 
     def settle(k, _):
         for upward in (True, False):
@@ -179,6 +201,7 @@
         scratch_shapes=[
             *[pltpu.VMEM((half, 2 * width), jnp.bfloat16)] * 4,
             pltpu.VMEM((rows, width), jnp.bfloat16),
+            pltpu.VMEM((2, chunk, 2 * width), jnp.float32),
             pltpu.SemaphoreType.DMA((8, half // chunk)),
         ],
         compiler_params=pltpu.CompilerParams(

time: 196 us -> 196 us (level)
  no operation moved by 1% of the time
where the time goes in v5:
time: 196 us; the launch traced here: 193 us
  Pallas kernels  175 us (89%)
  other arithmetic  11.7 us (6%)
  local copies, waits for them, and re-layouts  4.24 us (2%)
  matrix products  2.38 us (1%)
    pallas_call x1, Pallas kernels, expert_terms(): pl.pallas_call(functools.partial(expert_kernel, groups, chunk), out_shape...  92 us
    pallas_call x1, Pallas kernels, pick_rows(): pl.pallas_call(functools.partial(pick_kernel, groups, share, bits), out_s...  41.9 us
    pallas_call x1, Pallas kernels, total_rows(): pl.pallas_call(functools.partial(total_kernel, groups, share, bits), out_...  40.7 us

profile of v5, /device:TPU:0, one launch (start us, length us, event | category | flops | bytes accessed | tf_op | source)
XLA Modules:
  0.0 193.0 jit_solution(3513517392370015259)
XLA Ops:
  0.0 0.0 copy-start.4
  0.0 0.8 fusion.8
  0.8 0.3 reduce-window.9
  1.1 0.1 slice.7
  1.3 0.1 slice_reduce_fusion
  1.4 0.1 add_add_fusion
  1.5 0.7 reduce_sum.18
  2.2 0.7 fusion.6
  2.9 0.7 convert_element_type.60
  3.6 0.7 convert_element_type.64
  4.3 0.8 copy.14
  5.2 0.9 mul.45
  6.0 0.0 copy-done.4
  6.1 0.0 copy-start.2
  6.1 0.0 copy-start.3
  6.1 2.7 %fusion.1.down_ref = bf16[768,1024]{1,0:T(8,128)(2,1)S(1)} fusion(f32[96,8,8,128]{3,2,1,0:T(8,128)S(1)} %bitcast.33, bf16[768,1024]{1,0:T(8,128)(2,1)S(1)} %copy-done.4, bf16[768,4096]{1,0:T(8,128)(2,1)} %param.17, s32[]{:T(128)S(6)} %select_n.28), kind=kLoop, calls=%fused_computation.2 | loop fusion | flops 3932160 | bytes 7864324 | tf_op jit(solution)/shard_map/convert_element_type | solution.py:228
  8.8 0.0 copy-done.2
  8.8 0.0 copy-done.3
  8.9 2.9 %fusion.3 = (bf16[1024,768]{1,0:T(8,128)(2,1)S(1)}, bf16[1024,768]{1,0:T(8,128)(2,1)S(1)}) fusion(bf16[1024,768]{1,0:T(8,128)(2,1)S(1)} %copy-done.2, f32[8,768]{1,0:T(8,128)S(1)} %convert_element_type.64, bf16[4096,768]{1,0:T(8,128)(2,1)} %param.16, s32[]{:T(128)S(6)} %select_n.28, f32[8,768]{1,0:T(8,128)S(1)} %convert_element_type.60, ...), kind=kLoop, calls=%fused_computation.6 | loop fusion | flops 7864320 | bytes 9486340 | tf_op jit(solution)/shard_map/convert_element_type | solution.py:219
  11.8 0.0 copy-start.1
  11.8 1.9 pad_maximum_fusion.w_ref
  13.7 0.0 copy-done.1
  13.7 41.9 %shard_map.118 = (bf16[4,320,1024]{2,1,0:T(8,128)(2,1)S(1)}, bf16[4,320,512]{2,1,0:T(8,128)(2,1)S(1)}, f32[4,320,1]{2,1,0:T(8,128)S(1)}) custom-call(bf16[512,512]{1,0:T(8,128)(2,1)S(1)} %copy-done.1, f32[8,512]{1,0:T(8,128)S(1)} %select_maximum_fusion.route_ref), custom_call_target="tpu_custom_call" | custom-call | tf_op jit(solution)/shard_map/pallas_call | solution.py:576
  55.6 0.0 copy-start
  55.6 1.5 copy-done
  57.1 92.0 %shard_map.119 = bf16[1280,1024]{1,0:T(8,128)(2,1)S(1)} custom-call(bf16[1280,1024]{1,0:T(8,128)(2,1)} %bitcast.31, bf16[1024,1536]{1,0:T(8,128)(2,1)} %pad_maximum_fusion.w_ref, bf16[768,1024]{1,0:T(8,128)(2,1)S(1)} %fusion.1.down_ref, f32[1280,1]{1,0:T(8,128)S(1)} %bitcast.32), custom_call_target="tpu_custom_call" | custom-call | tf_op jit(solution)/shard_map/pallas_call | solution.py:196
  149.2 2.4 %fusion.9 = bf16[4,512,1024]{2,1,0:T(8,128)(2,1)S(1)} fusion(bf16[4,320,512]{2,1,0:T(8,128)(2,1)S(1)} %get-tuple-element.8, bf16[4,320,1024]{2,1,0:T(8,128)(2,1)S(1)} %bitcast.30), kind=kOutput, calls=%fused_computation.21 | convolution fusion | flops 1342177280 | bytes 8126464 | tf_op jit(solution)/shard_map/gsn,gsk->gnk/dot_general | solution.py:646
  151.5 40.7 %shard_map.120 = bf16[512,512]{1,0:T(8,128)(2,1)S(1)} custom-call(bf16[4,2,2,2,64,1024]{5,4,3,2,1,0:T(8,128)(2,1)S(1)} %bitcast.29), custom_call_target="tpu_custom_call" | custom-call | tf_op jit(solution)/shard_map/pallas_call | solution.py:386
  192.2 0.8 copy.18
  (4 shorter events, 0.1 us)
Async XLA Ops:
  0.0 6.0 %copy-start.4 = (bf16[768,1024]{1,0:T(8,128)(2,1)S(1)}, bf16[768,1024]{1,0:T(8,128)(2,1)}, u32[]{:S(2)}) copy-start(bf16[768,1024]{1,0:T(8,128)(2,1)} %param.22) | copy-start | bytes 4718596
  6.1 2.8 %copy-start.2 = (bf16[1024,768]{1,0:T(8,128)(2,1)S(1)}, bf16[1024,768]{1,0:T(8,128)(2,1)}, u32[]{:S(2)}) copy-start(bf16[1024,768]{1,0:T(8,128)(2,1)} %param.19) | copy-start | bytes 4718596
  6.1 2.8 %copy-start.3 = (bf16[1024,768]{1,0:T(8,128)(2,1)S(1)}, bf16[1024,768]{1,0:T(8,128)(2,1)}, u32[]{:S(2)}) copy-start(bf16[1024,768]{1,0:T(8,128)(2,1)} %param.18) | copy-start | bytes 4718596
  11.8 1.9 copy-start.1
  55.6 1.5 copy-start
